TPU v7x, 512 devices: a whole 4x4x16 slice. The times are simulated.
512 devices in a mesh: sec: 64 (over y, z), tp: 8 (over x, core).
Axes of the slice: x: 4, y: 4, z: 16, core: 2. Of those that a mesh axis runs over, the one named last changes fastest.
Arguments:
- ctx_q: bfloat16 [16384, 8192], P('sec', 'tp'), may hold values from -3 to 3
- ctx_kv: bfloat16 [2, 16384, 1024], P(None, 'sec', 'tp'), may hold values from -1000 to 1000
- anchor_kv: bfloat16 [2, 4096, 1024], P(None, 'sec', 'tp'), may hold values from -24 to 24
- counts: int32 [64], P('sec'), may hold values from 64 to 256, as said below
- offsets: int32 [64], P('sec'), may hold values from 0 to 128, as said below
- query_in: bfloat16 [256, 8192], P(None, 'sec'), may hold values from -6 to 6
- w_query: bfloat16 [8192, 8192], P('sec', 'tp'), may hold values from -0.03125 to 0.03125
- w_out: bfloat16 [8192, 8192], P('tp', 'sec'), may hold values from -0.1875 to 0.1875
Outputs:
- ctx_attn: bfloat16 [16384, 8192], P('sec', 'tp')
- result: bfloat16 [256, 8192], P('tp', 'sec')
Inputs may be any that keep to these rules, and one draw needn't show every extreme that they name: Each section's first counts[s] tokens are valid; some section is full in every draw. `offsets`: both ends of the range are taken by some section in every draw.
All inputs are finite; a program needn't handle non-finite values.
Results may differ from a plain program's by a relative error of at most 0.02.
The roundings to bfloat16 on the way count: a program that leaves them out, or rounds other values in their place, can miss the bound.
Values may be sent and summed in bfloat16 or wider, within the bound.
No kernel may reach another device: no remote copies, remote signals or barrier semaphores. Data moves between devices by JAX's collectives and lax.ppermute only.
A program may use at most 192 MiB of HBM per device.

v0:
```python
import math

import jax
import jax.numpy as jnp
from jax import lax
from jax.sharding import PartitionSpec as P

HD = 128


masked_score = -1e30


def merge_pair(first, second):
    first_max, first_sum, first_out = first
    second_max, second_sum, second_out = second
    joint_max = jnp.maximum(first_max, second_max)
    first_rate = jnp.exp(first_max - joint_max)
    second_rate = jnp.exp(second_max - joint_max)
    joint_sum = first_sum * first_rate + second_sum * second_rate
    joint_out = first_out * first_rate[..., None] + second_out * second_rate[..., None]
    return (joint_max, joint_sum, joint_out)


def partial_softmax(queries, key_rows, value_rows, visible):
    groups = key_rows.shape[-1] // HD
    key_heads = key_rows.reshape(key_rows.shape[0], groups, HD)
    value_heads = value_rows.reshape(value_rows.shape[0], groups, HD)
    scores = jnp.einsum(
        "rgpd,kgd->gprk", queries, key_heads, preferred_element_type=jnp.float32
    ) * HD ** (-0.5)
    scores = jnp.where(visible, scores, masked_score)
    row_max = scores.max(-1)
    weights = jnp.exp(scores - row_max[..., None])
    row_sum = weights.sum(-1)
    out_sum = jnp.einsum(
        "gprk,kgd->gprd",
        weights.astype(jnp.bfloat16),
        value_heads,
        preferred_element_type=jnp.float32,
    )
    return (row_max, row_sum, out_sum)


def attend_blocks(running, queries, key_rows, value_rows):
    length = key_rows.shape[0]
    block_len = math.gcd(length, 512)
    feature_len = key_rows.shape[-1]

    def one_block(state, blocks):
        return (merge_pair(state, partial_softmax(queries, blocks[0], blocks[1], True)), None)

    stacked = (
        key_rows.reshape(length // block_len, block_len, feature_len),
        value_rows.reshape(length // block_len, block_len, feature_len),
    )
    final_state, unused = lax.scan(one_block, running, stacked)
    return final_state


def body(ctx_q, ctx_kv, anchor_kv, counts, offsets, query_in, w_query, w_out):
    sec_rows = ctx_q.shape[0]
    groups = ctx_kv.shape[-1] // HD
    repeat = ctx_q.shape[-1] // (groups * HD)
    queries = ctx_q.reshape(sec_rows, groups, repeat, HD)
    positions = jnp.arange(sec_rows, dtype=jnp.int32)
    own_visible = (positions[None, :] < counts[0]) & (
        positions[None, :] <= positions[:, None] + offsets[0]
    )
    running = partial_softmax(queries, ctx_kv[0], ctx_kv[1], own_visible)
    gathered = lax.all_gather(anchor_kv, "sec", axis=1, tiled=True)
    running = attend_blocks(running, queries, gathered[0], gathered[1])
    context_max, context_sum, context_out = running
    ctx_attn = (
        jnp.transpose(context_out / context_sum[..., None], (2, 0, 1, 3))
        .reshape(sec_rows, -1)
        .astype(jnp.bfloat16)
    )
    partial_query = jnp.dot(query_in, w_query, preferred_element_type=jnp.float32)
    projected = lax.psum(partial_query, "sec").astype(jnp.bfloat16)
    query_rows = projected.shape[0]
    projected = projected.reshape(query_rows, groups, repeat, HD)
    cache_visible = positions[None, :] < counts[0]
    local_part = partial_softmax(projected, ctx_kv[0], ctx_kv[1], cache_visible)
    local_max, local_sum, local_out = local_part
    joint_max = lax.pmax(local_max, "sec")
    factor = jnp.exp(local_max - joint_max)
    joint_sum, joint_out = lax.psum((local_sum * factor, local_out * factor[..., None]), "sec")
    attended = (
        jnp.transpose(joint_out / joint_sum[..., None], (2, 0, 1, 3))
        .reshape(query_rows, -1)
        .astype(jnp.bfloat16)
    )
    result = lax.psum_scatter(
        jnp.dot(attended, w_out, preferred_element_type=jnp.float32).astype(jnp.bfloat16),
        "tp",
        scatter_dimension=0,
        tiled=True,
    )
    return (ctx_attn, result)


def solution(mesh):
    placed = (
        P("sec", "tp"),
        P(None, "sec", "tp"),
        P(None, "sec", "tp"),
        P("sec"),
        P("sec"),
        P(None, "sec"),
        P("sec", "tp"),
        P("tp", "sec"),
    )
    return jax.shard_map(
        body,
        mesh=mesh,
        in_specs=placed,
        out_specs=(P("sec", "tp"), P("tp", "sec")),
        check_vma=False,
    )
```

profile of v0, /device:TPU:1, one launch (start us, length us, event | category | flops | bytes accessed | tf_op | source)
XLA Modules:
  0.0 892.7 jit_solution(16102576181784058961)
XLA Ops:
  8.1 1.1 fusion.62
  9.2 240.7 %all-reduce.4 = bf16[256,1024]{1,0:T(8,128)(2,1)S(1)} all-reduce(f32[256,1024]{1,0:T(8,128)S(1)} %fusion.62), channel_id=1, replica_groups=mesh['sec'=64,'tp'=8] {'sec'}, use_global_device_ids=true, to_apply=%region_6.7 | all-reduce | flops 262144 | bytes 1572864 | tf_op jit(solution)/shard_map/psum | solution.py:80
  250.7 113.0 %pmax.7 = f32[1,8,256]{2,1,0:T(8,128)S(1)} all-reduce(f32[1,8,256]{2,1,0:T(8,128)S(1)} %bitcast.191), channel_id=1, replica_groups=mesh['sec'=64,'tp'=8] {'sec'}, use_global_device_ids=true, to_apply=%region_8.9 | all-reduce | flops 2048 | bytes 16384 | tf_op jit(solution)/shard_map/pmax | solution.py:86
  363.7 1.6 fusion.35
  365.4 0.7 all-gather.2.cloned.1.call-update
  367.3 114.4 %psum.23 = f32[8,256]{1,0:T(8,128)S(1)} all-reduce(f32[8,256]{1,0:T(8,128)S(1)} %get-tuple-element.71), channel_id=1, replica_groups=mesh['sec'=64,'tp'=8] {'sec'}, use_global_device_ids=true, to_apply=%region_11.12 | all-reduce | flops 2048 | bytes 16384 | tf_op jit(solution)/shard_map/psum | solution.py:88
  483.2 218.2 %all-reduce.3.cloned.1.call-done = f32[1,8,256,128]{3,2,1,0:T(8,128)} async-done(((f32[1,8,256,128]{3,2,1,0:T(8,128)}), f32[1,8,256,128]{3,2,1,0:T(8,128)}) %all-reduce.3.cloned.1.call-update) | async-done | bytes 1048592 | tf_op jit(solution)/shard_map/psum | solution.py:88
  701.4 1.6 fusion.47
  703.2 1.0 convolution_convert_fusion
  704.2 137.3 %all-gather.2.cloned.1.call-done = bf16[2,4096,128]{2,1,0:T(8,128)(2,1)} async-done(((bf16[2,64,128]{2,1,0:T(8,128)(2,1)}), bf16[2,4096,128]{2,1,0:T(8,128)(2,1)}) %all-gather.2.cloned.1.call-update) | async-done | bytes 2097168 | tf_op jit(solution)/shard_map/all_gather | solution.py:71
  841.4 2.7 fusion.59
  844.1 33.0 %while.14 = (s32[]{:T(128)}, f32[1,8,256]{2,1,0:T(8,128)S(1)}, f32[1,8,256]{2,1,0:T(8,128)S(1)}, f32[1,8,256,128]{3,2,1,0:T(8,128)S(1)}, bf16[8,512,128]{2,1,0:T...) while((s32[]{:T(128)}, f32[1,8,256]{2,1,0:T(8,128)S(1)}, ...), condition=%wide.region_5.6_spmd, body=%wide.region_2.5_spmd.sunk | while | flops 546056192 | bytes 15622245 | solution.py:57
  844.1 1.6 bitcast_reduce_fusion.2
  845.7 0.7 fusion.78
  846.5 1.7 fusion.80
  848.2 1.6 bitcast_reduce_fusion.2
  849.9 0.7 fusion.78
  850.6 1.7 fusion.80
  852.4 1.6 bitcast_reduce_fusion.2
  854.7 1.7 fusion.80
  856.5 1.6 bitcast_reduce_fusion.2
  858.9 1.7 fusion.80
  860.6 1.6 bitcast_reduce_fusion.2
  863.0 1.7 fusion.80
  864.8 1.6 bitcast_reduce_fusion.2
  867.1 1.7 fusion.80
  868.9 1.6 bitcast_reduce_fusion.2
  871.3 1.7 fusion.80
  873.0 1.6 bitcast_reduce_fusion.2
  875.4 1.7 fusion.80
  877.9 0.9 copy.44
  878.8 7.4 reduce-scatter.2.cloned.1.call-done
  (61 shorter events, 8.3 us)
Async XLA Ops:
  7.2 1.0 copy-start
  7.2 242.7 %copy-start.2 = (bf16[2,256,128]{2,1,0:T(8,128)(2,1)S(1)}, bf16[2,256,128]{2,1,0:T(8,128)(2,1)}, u32[]{:S(2)}) copy-start(bf16[2,256,128]{2,1,0:T(8,128)(2,1)} %param.11) | copy-start | bytes 393220
  7.2 694.2 %all-reduce.3.cloned.1.call-start = ((), (), s32[]{:S(2)}) async-start(), calls=%async_computation.2 | async-start | bytes 2097152 | tf_op jit(solution)/shard_map/psum | solution.py:88
  8.1 242.3 %copy-start.4 = (pred[256]{0:T(512)(128)(4,1)}, pred[256]{0:T(512)(128)(4,1)S(1)}, u32[]{:S(2)}) copy-start(pred[256]{0:T(512)(128)(4,1)S(1)} %iota_compare_fusion.1) | copy-start | bytes 772
  363.7 3.1 copy-start.1
  365.4 116.4 %copy-start.5 = (pred[256]{0:T(512)(128)(4,1)S(1)}, pred[256]{0:T(512)(128)(4,1)}, u32[]{:S(2)}) copy-start(pred[256]{0:T(512)(128)(4,1)} %copy-done.4) | copy-start | bytes 772
  365.4 476.1 %all-gather.2.cloned.1.call-start = ((), (), s32[]{:S(2)}) async-start(), calls=%async_computation.1 | async-start | bytes 2129920 | tf_op jit(solution)/shard_map/all_gather | solution.py:71
  366.1 520.1 %reduce-scatter.2.cloned.1.call-start = ((), (), s32[]{:S(2)}) async-start(), calls=%async_computation.3 | async-start | bytes 73728 | tf_op jit(solution)/shard_map/reduce_scatter | solution.py:94
  483.2 220.0 %copy-start.3 = (bf16[1024,128]{1,0:T(8,128)(2,1)S(1)}, bf16[1024,128]{1,0:T(8,128)(2,1)}, u32[]{:S(2)}) copy-start(bf16[1024,128]{1,0:T(8,128)(2,1)} %param.17) | copy-start | bytes 786436
Sparse Core Ops, SparseCore 0:
  365.5 335.8 all-reduce.2
  704.8 136.6 all-gather.1
  845.0 41.1 reduce-scatter.1
where the time goes:
time: 894 us; the launch traced here: 893 us
  blocking collectives  468 us (52%)
  waiting for transfers between devices  364 us (41%)
  matrix products  32 us (4%)
  between operations  15.3 us (2%)
    psum x1, blocking collectives, body(): projected = lax.psum(partial_query, 'sec').astype(jnp.bfloat16)  241 us
    psum x1, waiting for transfers between devices, body(): lax.psum((local_sum * factor, local_out * factor[..., None]), 'sec')  218 us
    all_gather x1, waiting for transfers between devices, body(): gathered = lax.all_gather(anchor_kv, 'sec', axis=1, tiled=True)  137 us
    psum x1, blocking collectives, body(): lax.psum((local_sum * factor, local_out * factor[..., None]), 'sec')  114 us
    pmax x1, blocking collectives, body(): joint_max = lax.pmax(local_max, 'sec')  113 us
  transfers between devices with their start and end apart: 3, of which 3 were waited for; matrix products, arithmetic and copies ran while one was open for 5% of the time, Pallas kernels for 0%

commit v1 on v0

v1 whole, which is shorter than its diff:
```python
import functools

import jax
import jax.numpy as jnp
from jax import lax
from jax.experimental import pallas as pl
from jax.experimental.pallas import tpu as pltpu
from jax.sharding import Mesh, PartitionSpec as P

HD = 128
SCALE = HD ** (-0.5)
RATE = SCALE * 1.4426950408889634
masked_score = -1e30
VMEM_LIMIT = 48 * 1024 * 1024


def score_dot(queries, keys):
    return lax.dot_general(
        queries, keys, (((1,), (1,)), ((), ())), preferred_element_type=jnp.float32
    )


def merge_chunk(state, scores, values):
    chunk_max = jnp.max(scores, axis=1, keepdims=True)
    if state is None:
        weights = jnp.exp2((scores - chunk_max) * RATE)
        total = jnp.sum(weights, axis=1, keepdims=True)
        out = jnp.dot(weights.astype(jnp.bfloat16), values, preferred_element_type=jnp.float32)
        return chunk_max, total, out
    row_max, total, out = state
    joint = jnp.maximum(row_max, chunk_max)
    rate = jnp.exp2((row_max - joint) * RATE)
    weights = jnp.exp2((scores - joint) * RATE)
    total = total * rate + jnp.sum(weights, axis=1, keepdims=True)
    part = jnp.dot(weights.astype(jnp.bfloat16), values, preferred_element_type=jnp.float32)
    return joint, total, out * rate + part


def context_kernel(bounds, q_ref, own_ref, anchor_ref, *rest):
    out_ref = rest[-1]
    rows = q_ref.shape[0]
    queries = jnp.concatenate([q_ref[:, :HD], q_ref[:, HD:]], axis=0)
    scores = score_dot(queries, own_ref[0])
    key = lax.broadcasted_iota(jnp.int32, scores.shape, 1)
    row = lax.broadcasted_iota(jnp.int32, scores.shape, 0) & (rows - 1)
    visible = (key < bounds[0]) & (key <= row + bounds[1])
    state = merge_chunk(None, jnp.where(visible, scores, masked_score), own_ref[1])
    for part in range(anchor_ref.shape[0]):
        keys = anchor_ref[part, :, 0].reshape(-1, HD)
        values = anchor_ref[part, :, 1].reshape(-1, HD)
        state = merge_chunk(state, score_dot(queries, keys), values)
    mixed = state[2] / state[1]
    out_ref[:, :HD] = mixed[:rows].astype(jnp.bfloat16)
    out_ref[:, HD:] = mixed[rows:].astype(jnp.bfloat16)


def context_attention(queries, own, anchors, bounds, previous, index):
    rows, width = queries.shape
    columns = pl.BlockSpec((rows, 2 * HD), lambda i, b: (0, index))
    whole = lambda array: pl.BlockSpec(array.shape, lambda i, b: (0,) * array.ndim)
    operands = [queries, own, anchors]
    in_specs = [columns, whole(own), whole(anchors)]
    aliases = {}
    if previous is not None:
        operands.append(previous)
        in_specs.append(pl.BlockSpec(memory_space=pl.ANY))
        aliases = {4: 0}
    keys = own.shape[1] + anchors.size // (2 * HD)
    return pl.pallas_call(
        context_kernel,
        grid_spec=pltpu.PrefetchScalarGridSpec(
            num_scalar_prefetch=1, grid=(1,), in_specs=in_specs, out_specs=columns
        ),
        out_shape=jax.ShapeDtypeStruct((rows, width), jnp.bfloat16),
        input_output_aliases=aliases,
        compiler_params=pltpu.CompilerParams(vmem_limit_bytes=VMEM_LIMIT),
        cost_estimate=pl.CostEstimate(
            flops=16 * rows * keys * HD, bytes_accessed=2 * anchors.size, transcendentals=2 * rows * keys
        ),
    )(bounds, *operands)


def pack_kernel(q_ref, w_ref, out_ref):
    parts, qrows = out_ref.shape[0], q_ref.shape[0]
    depth = w_ref.shape[0]
    heads = w_ref.shape[1] // (parts * HD)
    for part in range(parts):
        out_ref[part, :qrows] = q_ref[...]
        for head in range(heads):
            start = (part * heads + head) * HD
            out_ref[part, qrows + head * depth : qrows + (head + 1) * depth] = w_ref[:, start : start + HD]


def project_kernel(depth, share, in_ref, out_ref):
    nl, rows, width = out_ref.shape
    qrows = nl * rows
    for head in range(width // HD):
        total = 0.0
        for part in range(in_ref.shape[0]):
            start = qrows + head * depth
            total = total + jnp.dot(
                in_ref[part, :qrows],
                in_ref[part, start : start + depth],
                preferred_element_type=jnp.float32,
            )
        for high in range(rows // share):
            for low in range(nl):
                row = (high * nl + low) * share
                out_ref[low, high * share : (high + 1) * share, head * HD : (head + 1) * HD] = total[
                    row : row + share
                ]


def across(row, size):
    return jnp.transpose(jnp.broadcast_to(row, (size, size)))


def section_kernel(length, q_ref, cache_ref, out_ref):
    heads = q_ref.shape[1] // HD
    size = out_ref.shape[1] - 8
    queries = jnp.concatenate([q_ref[:, head * HD : (head + 1) * HD] for head in range(heads)], axis=0)
    state = None
    for first in range(0, cache_ref.shape[0], 4):
        scores, values = [], []
        for part in range(first, first + 4):
            score = score_dot(queries, cache_ref[part, :length])
            values.append(cache_ref[part, length : 2 * length])
            count = cache_ref[part, 2 * length : 2 * length + 16].astype(jnp.float32)
            key = lax.broadcasted_iota(jnp.int32, score.shape, 1).astype(jnp.float32)
            scores.append(jnp.where(key < count[:1, :1], score, masked_score))
        state = merge_chunk(state, jnp.concatenate(scores, axis=1), jnp.concatenate(values, axis=0))
    row_max, total, out = state
    row_max = jnp.transpose(jnp.broadcast_to(row_max, (size, HD)))
    total = jnp.transpose(jnp.broadcast_to(total, (size, HD)))
    stats = jnp.concatenate([row_max[:4], total[:4]], axis=0)
    for copy in range(out_ref.shape[0]):
        out_ref[copy, :size] = out
        out_ref[copy, size:] = stats


def finish_kernel(in_ref, out_ref):
    parts = in_ref.shape[0]
    size = in_ref.shape[1] - 8
    rows = out_ref.shape[1]
    maxes = [in_ref[part, size : size + 1] for part in range(parts)]
    joint = functools.reduce(jnp.maximum, maxes)
    rates = [jnp.exp2((other - joint) * RATE) for other in maxes]
    total = 0.0
    for part in range(parts):
        total = total + rates[part] * in_ref[part, size + 4 : size + 5]
    mixed = 0.0
    for part in range(parts):
        mixed = mixed + across(rates[part], size) * in_ref[part, :size]
    mixed = (mixed / across(total, size)).astype(jnp.bfloat16)
    for copy in range(out_ref.shape[0]):
        for head in range(size // rows):
            out_ref[copy, :, head * HD : (head + 1) * HD] = mixed[head * rows : (head + 1) * rows]


def output_kernel(share, att_ref, w_ref, out_ref):
    ny, nl, each, width = att_ref.shape
    rows = out_ref.shape[1]
    total = 0.0
    for part in range(ny):
        total = total + jnp.dot(
            att_ref[part].reshape(nl * each, width),
            w_ref[part * width : (part + 1) * width],
            preferred_element_type=jnp.float32,
        )
    for low in range(nl):
        for high in range(each // share):
            source = low * each + high * share
            target = (high * nl + low) * share
            offset = target % rows
            out_ref[target // rows, offset : offset + share] = total[source : source + share]


def spread(block, size):
    return jnp.broadcast_to(block[None], (size,) + block.shape)


def solution(mesh):
    ny, nh, nl, nx, nc = 4, 4, 4, 4, 2
    if mesh.shape["sec"] != ny * nh * nl:
        ny, nh, nl, nx, nc = 2, 2, 2, 2, 2
    nz, nt = nh * nl, nx * nc
    fine = Mesh(mesh.devices.reshape(ny, nh, nl, nx, nc), ("y", "h", "l", "x", "c"))
    sec, tp = ("y", "h", "l"), ("x", "c")

    def swap(array, axis):
        return lax.all_to_all(array, axis, 0, 0, tiled=True)

    def double(block, distance):
        pairs = [(z, z ^ distance) for z in range(nz)]
        return jnp.concatenate([block, lax.ppermute(block, ("h", "l"), pairs)], axis=0)

    def body(ctx_q, ctx_kv, anchor_kv, counts, offsets, query_in, w_query, w_out):
        rows = ctx_q.shape[0]
        heads = ctx_q.shape[1] // HD
        qrows, depth = query_in.shape
        part_heads = heads // ny
        width = part_heads * HD
        share = qrows // nz
        bf16, f32 = jnp.bfloat16, jnp.float32
        tie = lax.optimization_barrier

        def kernel(body, shape, dtype, *operands, **kwargs):
            return pl.pallas_call(
                body,
                out_shape=jax.ShapeDtypeStruct(shape, dtype),
                compiler_params=pltpu.CompilerParams(vmem_limit_bytes=VMEM_LIMIT),
                **kwargs,
            )(*operands)

        each = nh * share
        distances = [nz >> (step + 1) for step in range(nz.bit_length() - 1)]
        anchors = anchor_kv[None]

        packed = kernel(pack_kernel, (ny, qrows + part_heads * depth, HD), bf16, query_in, w_query)
        cache = jnp.concatenate(
            [ctx_kv.reshape(2 * rows, HD), jnp.broadcast_to(counts[0].astype(bf16), (16, HD))], axis=0
        )
        packed, cache = tie((packed, cache))
        packed = swap(packed, "y")
        window = [cache[None]]
        for shift in (1, -1, 2)[: nl - 1]:
            pairs = [(z, (z + shift) % nz) for z in range(nz)]
            window.append(lax.ppermute(cache[None], ("h", "l"), pairs))
        packed, window = tie((packed, window))
        caches = lax.all_gather(jnp.concatenate(window, axis=0), "y", axis=0, tiled=True)

        partial = kernel(
            functools.partial(project_kernel, depth, share), (nl, each, width), f32, packed
        )
        partial = swap(partial, "l")
        for distance in distances[:-3]:
            anchors = double(anchors, distance)
        partial, anchors = tie((partial, anchors))
        partial = swap(spread(partial.sum(0), nh), "h")
        for distance in distances[-3:-1]:
            anchors = double(anchors, distance)
        partial, anchors = tie((partial, anchors))
        projected = partial.sum(0).astype(bf16)
        anchors = double(anchors, distances[-1])

        state = kernel(
            functools.partial(section_kernel, rows),
            (nh, part_heads * each + 8, HD),
            f32,
            projected,
            caches,
        )
        state, anchors = tie((state, anchors))
        anchors = lax.all_gather(anchors, "y", axis=0, tiled=False)
        state = swap(state, "h")
        attended = kernel(finish_kernel, (nl, each, width), bf16, state)
        attended = swap(attended, "l")

        bounds = jnp.stack([counts[0], offsets[0]])
        attend = lambda previous, index: context_attention(ctx_q, ctx_kv, anchors, bounds, previous, index)
        attended, anchors = tie((attended, anchors))
        attended = swap(spread(attended, ny), "y")
        ctx_attn = attend(None, 0)
        attended, ctx_attn = tie((attended, ctx_attn))
        product = kernel(
            functools.partial(output_kernel, share), (nt, qrows // nt, HD), f32, attended, w_out
        )
        product, ctx_attn = tie((product, ctx_attn))
        product = swap(product, tp)
        for index in range(1, heads // 2):
            ctx_attn = attend(ctx_attn, index)
        result = product.sum(0).astype(bf16)
        return (ctx_attn, result)

    placed = (
        P(sec, tp),
        P(None, sec, tp),
        P(None, sec, tp),
        P(sec),
        P(sec),
        P(None, sec),
        P(sec, tp),
        P(tp, sec),
    )
    return jax.shard_map(
        body,
        mesh=fine,
        in_specs=placed,
        out_specs=(P(sec, tp), P(tp, sec)),
        check_vma=False,
    )
```

time: 894 us -> 191 us (0.21)
  blocking collectives: 468 us -> 43.3 us
  waiting for transfers between devices: 364 us -> 26.8 us
  starting transfers between devices: 0.12 us -> 72 us
  matrix products: 32 us -> 0 us
  Pallas kernels: 0 us -> 23 us
    psum x2 -> x0, blocking collectives: 355 us -> none  [the longest x1 241 us: body(): projected = lax.psum(partial_query, 'sec').astype(jnp.bfloat16)]
    psum x1 -> x0, waiting for transfers between devices: 218 us -> none  [body(): lax.psum((local_sum * factor, local_out * factor[..., None]), 'sec')]
    all_gather x1 -> x2, waiting for transfers between devices: 137 us -> 2.7 us  [the longest x1 2.7 us: body(): anchors = lax.all_gather(anchors, 'y', axis=0, tiled=False)]
    pmax x1 -> x0, blocking collectives: 113 us -> none  [body(): joint_max = lax.pmax(local_max, 'sec')]
    all_to_all x0 -> x2, blocking collectives: none -> 43.3 us  [swap(): return lax.all_to_all(array, axis, 0, 0, tiled=True)]
    ppermute x0 -> x7, starting transfers between devices: none -> 42.5 us  [the longest x4 27.6 us: double(): lax.ppermute(block, ('h', 'l'), pairs)]
    dot_general x22 -> x0, matrix products: 32 us -> none  [the longest x10 16 us: partial_softmax(): jnp.einsum('gprk,kgd->gprd', weights.astype(jnp.bfloat16), value_heads, p...]
    all_to_all x0 -> x5, starting transfers between devices: none -> 29.5 us  [swap(): return lax.all_to_all(array, axis, 0, 0, tiled=True)]
  transfers between devices with their start and end apart: 3 -> 14, of which waited for: 3 -> 8; matrix products, arithmetic and copies ran while one was open for 5% -> 1% of each run, Pallas kernels for 0% -> 5%
where the time goes in v1:
time: 191 us
  starting transfers between devices  72 us (38%)
  blocking collectives  43.3 us (23%)
  waiting for transfers between devices  26.8 us (14%)
  Pallas kernels  23 us (12%)
  between operations  15.5 us (8%)
  local copies, waits for them, and re-layouts  7.49 us (4%)
  other arithmetic  2.5 us (1%)
    all_to_all x2, blocking collectives, swap(): return lax.all_to_all(array, axis, 0, 0, tiled=True)  43.3 us
    all_to_all x5, starting transfers between devices, swap(): return lax.all_to_all(array, axis, 0, 0, tiled=True)  29.5 us
    ppermute x4, starting transfers between devices, double(): lax.ppermute(block, ('h', 'l'), pairs)  27.6 us
    pallas_call x4, Pallas kernels, context_attention(): pl.pallas_call(context_kernel, grid_spec=pltpu.PrefetchScalarGridSpec(num...  18.5 us
    ppermute x4, waiting for transfers between devices, double(): lax.ppermute(block, ('h', 'l'), pairs)  18.3 us
    ppermute x3, starting transfers between devices, body(): window.append(lax.ppermute(cache[None], ('h', 'l'), pairs))  15 us
    ppermute x3, waiting for transfers between devices, body(): window.append(lax.ppermute(cache[None], ('h', 'l'), pairs))  5.04 us
    unnamed x18, local copies, waits for them, and re-layouts  5.01 us
  transfers between devices with their start and end apart: 14, of which 8 were waited for; matrix products, arithmetic and copies ran while one was open for 1% of the time, Pallas kernels for 5%

profile of v1, /device:TPU:1, one launch (start us, length us, event | category | flops | bytes accessed | tf_op | source)
XLA Modules:
  0.0 190.5 jit_solution(16279434767345284551)
XLA Ops:
  7.8 0.9 concatenate.19
  8.7 0.9 copy-done.2
  11.4 5.1 %all-to-all-start = ((bf16[4,512,128]{2,1,0:T(8,128)(2,1)}), bf16[4,512,128]{2,1,0:T(8,128)(2,1)S(1)}, u32[]{:S(2)}, u32[]{:S(2)}) async-start(bf16[4,512,128]{2,1,0:T(8,128)(2,1)} %shard_map.95), calls=%async_computation | async-start | bytes 1048576 | tf_op jit(solution)/shard_map/all_to_all | solution.py:191
  16.5 4.9 %collective-permute-start.2 = (bf16[1,528,128]{2,1,0:T(8,128)(2,1)S(1)}, bf16[1,528,128]{2,1,0:T(8,128)(2,1)S(1)}, u32[]{:S(2)}, u32[]{:S(2)}) collective-permute-start(bf16[1,528,128]{2,1,0:T(8,128)(2,1)S(1)} %bitcast.10), channel_id=1, source_target_pairs={{0,16},{8,24},{16,32},{24,40},{32,48},{40,56},{48,64},{56,72},{64,... | collective-permute-start | bytes 405512 | tf_op jit(solution)/shard_map/ppermute | solution.py:228
  21.4 8.1 %collective-permute-start.1 = (bf16[1,528,128]{2,1,0:T(8,128)(2,1)S(1)}, bf16[1,528,128]{2,1,0:T(8,128)(2,1)S(1)}, u32[]{:S(2)}, u32[]{:S(2)}) collective-permute-start(bf16[1,528,128]{2,1,0:T(8,128)(2,1)S(1)} %bitcast.11), channel_id=1, source_target_pairs={{0,120},{8,0},{16,8},{24,16},{32,24},{40,32},{48,40},{56,48},{64,5... | collective-permute-start | bytes 405512 | tf_op jit(solution)/shard_map/ppermute | solution.py:228
  29.6 1.9 %collective-permute-start = (bf16[1,528,128]{2,1,0:T(8,128)(2,1)S(1)}, bf16[1,528,128]{2,1,0:T(8,128)(2,1)S(1)}, u32[]{:S(2)}, u32[]{:S(2)}) collective-permute-start(bf16[1,528,128]{2,1,0:T(8,128)(2,1)S(1)} %bitcast.12), channel_id=1, source_target_pairs={{0,8},{8,16},{16,24},{24,32},{32,40},{40,48},{48,56},{56,64},{64,7... | collective-permute-start | bytes 405512 | tf_op jit(solution)/shard_map/ppermute | solution.py:228
  31.7 4.8 %collective-permute-done = bf16[1,528,128]{2,1,0:T(8,128)(2,1)S(1)} collective-permute-done((bf16[1,528,128]{2,1,0:T(8,128)(2,1)S(1)}, bf16[1,528,128]{2,1,0:T(8,128)(2,1)S(1)}, u32[]{:S(2)}, u32[]{:S(2)}) %collective-permute-start) | collective-permute-done | bytes 135200 | tf_op jit(solution)/shard_map/ppermute | solution.py:228
  36.6 0.9 pad_maximum_fusion
  37.5 1.0 shard_map.96
  38.5 3.4 %all-to-all-start.1 = ((f32[4,64,256]{2,1,0:T(8,128)}), f32[4,64,256]{2,1,0:T(8,128)S(1)}, u32[]{:S(2)}, u32[]{:S(2)}) async-start(f32[4,64,256]{2,1,0:T(8,128)} %shard_map.96), calls=%async_computation.1 | async-start | bytes 524288 | tf_op jit(solution)/shard_map/all_to_all | solution.py:191
  41.9 9.3 %collective-permute-start.3 = (bf16[1,2,64,128]{3,2,1,0:T(8,128)(2,1)S(1)}, bf16[1,2,64,128]{3,2,1,0:T(8,128)(2,1)S(1)}, u32[]{:S(2)}, u32[]{:S(2)}) collective-permute-start(bf16[1,2,64,128]{3,2,1,0:T(8,128)(2,1)S(1)} %bitcast.14), channel_id=1, source_target_pairs={{0,64},{8,72},{16,80},{24,88},{32,96},{40,104},{48,112},{56,120},{... | collective-permute-start | bytes 98312 | tf_op jit(solution)/shard_map/ppermute | solution.py:195
  51.2 4.5 %collective-permute-done.3 = bf16[1,2,64,128]{3,2,1,0:T(8,128)(2,1)S(1)} collective-permute-done((bf16[1,2,64,128]{3,2,1,0:T(8,128)(2,1)S(1)}, bf16[1,2,64,128]{3,2,1,0:T(8,128)(2,1)S(1)}, u32[]{:S(2)}, u32[]{:S(2)}) %collective-permute-start.3) | collective-permute-done | bytes 32800 | tf_op jit(solution)/shard_map/ppermute | solution.py:195
  56.5 8.2 %all-to-all-start.2 = ((f32[4,64,256]{2,1,0:T(8,128)}), f32[4,64,256]{2,1,0:T(8,128)S(1)}, u32[]{:S(2)}, u32[]{:S(2)}) async-start(f32[4,64,256]{2,1,0:T(8,128)} %broadcast_in_dim.10), calls=%async_computation.2 | async-start | bytes 524288 | tf_op jit(solution)/shard_map/all_to_all | solution.py:191
  64.8 7.3 %collective-permute-start.4 = (bf16[2,2,64,128]{3,2,1,0:T(8,128)(2,1)S(1)}, bf16[2,2,64,128]{3,2,1,0:T(8,128)(2,1)S(1)}, u32[]{:S(2)}, u32[]{:S(2)}) collective-permute-start(bf16[2,2,64,128]{3,2,1,0:T(8,128)(2,1)S(1)} %pad_maximum_fusion.4), channel_id=1, source_target_pairs={{0,32},{8,40},{16,48},{24,56},{32,0},{40,8},{48,16},{56,24},{64,96... | collective-permute-start | bytes 196616 | tf_op jit(solution)/shard_map/ppermute | solution.py:195
  72.0 5.1 %collective-permute-done.4 = bf16[2,2,64,128]{3,2,1,0:T(8,128)(2,1)S(1)} collective-permute-done((bf16[2,2,64,128]{3,2,1,0:T(8,128)(2,1)S(1)}, bf16[2,2,64,128]{3,2,1,0:T(8,128)(2,1)S(1)}, u32[]{:S(2)}, u32[]{:S(2)}) %collective-permute-start.4) | collective-permute-done | bytes 65568 | tf_op jit(solution)/shard_map/ppermute | solution.py:195
  77.2 4.7 %collective-permute-start.5 = (bf16[4,2,64,128]{3,2,1,0:T(8,128)(2,1)S(1)}, bf16[4,2,64,128]{3,2,1,0:T(8,128)(2,1)S(1)}, u32[]{:S(2)}, u32[]{:S(2)}) collective-permute-start(bf16[4,2,64,128]{3,2,1,0:T(8,128)(2,1)S(1)} %pad_maximum_fusion.3), channel_id=1, source_target_pairs={{0,16},{8,24},{16,0},{24,8},{32,48},{40,56},{48,32},{56,40},{64,80... | collective-permute-start | bytes 393224 | tf_op jit(solution)/shard_map/ppermute | solution.py:195
  81.9 4.0 %collective-permute-done.5 = bf16[4,2,64,128]{3,2,1,0:T(8,128)(2,1)S(1)} collective-permute-done((bf16[4,2,64,128]{3,2,1,0:T(8,128)(2,1)S(1)}, bf16[4,2,64,128]{3,2,1,0:T(8,128)(2,1)S(1)}, u32[]{:S(2)}, u32[]{:S(2)}) %collective-permute-start.5) | collective-permute-done | bytes 131104 | tf_op jit(solution)/shard_map/ppermute | solution.py:195
  86.0 6.2 %collective-permute-start.6 = (bf16[8,2,64,128]{3,2,1,0:T(8,128)(2,1)S(1)}, bf16[8,2,64,128]{3,2,1,0:T(8,128)(2,1)S(1)}, u32[]{:S(2)}, u32[]{:S(2)}) collective-permute-start(bf16[8,2,64,128]{3,2,1,0:T(8,128)(2,1)S(1)} %pad_maximum_fusion.2), channel_id=1, source_target_pairs={{0,8},{8,0},{16,24},{24,16},{32,40},{40,32},{48,56},{56,48},{64,72... | collective-permute-start | bytes 786440 | tf_op jit(solution)/shard_map/ppermute | solution.py:195
  92.2 4.7 %collective-permute-done.6 = bf16[8,2,64,128]{3,2,1,0:T(8,128)(2,1)S(1)} collective-permute-done((bf16[8,2,64,128]{3,2,1,0:T(8,128)(2,1)S(1)}, bf16[8,2,64,128]{3,2,1,0:T(8,128)(2,1)S(1)}, u32[]{:S(2)}, u32[]{:S(2)}) %collective-permute-start.6) | collective-permute-done | bytes 262176 | tf_op jit(solution)/shard_map/ppermute | solution.py:195
  97.7 1.6 copy-done
  99.3 1.5 shard_map.97
  100.9 34.0 %all_to_all.35.in_ref = f32[4,136,128]{2,1,0:T(8,128)S(1)} all-to-all(f32[4,136,128]{2,1,0:T(8,128)S(1)} %shard_map.97), channel_id=1, replica_groups=mesh['y'=4,'h'=4,'l'=4,'x'=4,'c'=2] {'h'}, dimensions={0} | all-to-all | bytes 557056 | tf_op jit(solution)/shard_map/all_to_all | solution.py:191
  135.1 9.3 %all_to_all.36 = bf16[4,64,256]{2,1,0:T(8,128)(2,1)S(1)} all-to-all(bf16[4,64,256]{2,1,0:T(8,128)(2,1)S(1)} %shard_map.98), channel_id=1, replica_groups=mesh['y'=4,'h'=4,'l'=4,'x'=4,'c'=2] {'l'}, dimensions={0} | all-to-all | bytes 262144 | tf_op jit(solution)/shard_map/all_to_all | solution.py:191
  144.4 2.7 %all-gather.6.cloned.1.call-done = bf16[64,2,64,128]{3,2,1,0:T(8,128)(2,1)} async-done(((bf16[16,2,64,128]{3,2,1,0:T(8,128)(2,1)}), bf16[64,2,64,128]{3,2,1,0:T(8,128)(2,1)}) %all-gather.6.cloned.1.call-update) | async-done | bytes 2097168 | tf_op jit(solution)/shard_map/all_gather | solution.py:254
  147.9 3.6 %all-to-all-start.5 = ((bf16[4,4,64,256]{3,2,1,0:T(8,128)(2,1)}), bf16[4,4,64,256]{3,2,1,0:T(8,128)(2,1)S(1)}, u32[]{:S(2)}, u32[]{:S(2)}) async-start(bf16[4,4,64,256]{3,2,1,0:T(8,128)(2,1)} %broadcast_in_dim.11), calls=%async_computation.5 | async-start | bytes 1048576 | tf_op jit(solution)/shard_map/all_to_all | solution.py:191
  152.3 1.6 copy-done.5
  153.9 4.6 %shard_map.99.rest_0_ = bf16[256,1024]{1,0:T(8,128)(2,1)} custom-call(s32[2]{0:T(128)S(1)} %pad_add_fusion.bounds, bf16[256,1024]{1,0:T(8,128)(2,1)S(1)} %copy-done.7, bf16[2,256,128]{2,1,0:T(8,128)(2,1)S(1)} %copy-done.3, bf16[4,16,2,64,128]{4,3,2,1,0:T(8,128)(2,1)S(1)} %bitcast.6), custom_call_target="tpu_custom_call" | custom-call | flops 2281701376 | bytes 2097152 | tf_op jit(solution)/shard_map/pallas_call | solution.py:69
  158.6 0.9 shard_map.100
  159.5 4.6 %shard_map.101.rest_0_ = bf16[256,1024]{1,0:T(8,128)(2,1)} custom-call(s32[2]{0:T(128)S(1)} %pad_add_fusion.bounds, bf16[256,1024]{1,0:T(8,128)(2,1)S(1)} %copy-done.7, bf16[2,256,128]{2,1,0:T(8,128)(2,1)S(1)} %copy-done.3, bf16[4,16,2,64,128]{4,3,2,1,0:T(8,128)(2,1)S(1)} %bitcast.7, bf16[256,1024]{1,0:T(8,128)(2,1)} %shard_map.99.rest_0_), custom_call_target="tpu_custom_call", output_to_operand_aliasing={{}: (4, {})} | custom-call | flops 2281701376 | bytes 2097152 | tf_op jit(solution)/shard_map/pallas_call | solution.py:69
  164.1 4.6 %shard_map.102.rest_0_ = bf16[256,1024]{1,0:T(8,128)(2,1)} custom-call(s32[2]{0:T(128)S(1)} %pad_add_fusion.bounds, bf16[256,1024]{1,0:T(8,128)(2,1)S(1)} %copy-done.7, bf16[2,256,128]{2,1,0:T(8,128)(2,1)S(1)} %copy-done.3, bf16[4,16,2,64,128]{4,3,2,1,0:T(8,128)(2,1)S(1)} %bitcast.8, ...), custom_call_target="tpu_custom_call", output_to_operand_aliasing={{}: (4, {})} | custom-call | flops 2281701376 | bytes 2097152 | tf_op jit(solution)/shard_map/pallas_call | solution.py:69
  168.7 9.1 %all-to-all-start.6 = ((f32[8,32,128]{2,1,0:T(8,128)}), f32[8,32,128]{2,1,0:T(8,128)S(1)}, u32[]{:S(2)}, u32[]{:S(2)}) async-start(f32[8,32,128]{2,1,0:T(8,128)} %shard_map.100), calls=%async_computation.6 | async-start | bytes 262144 | tf_op jit(solution)/shard_map/all_to_all | solution.py:191
  177.8 4.6 %shard_map.103 = bf16[256,1024]{1,0:T(8,128)(2,1)} custom-call(s32[2]{0:T(128)S(1)} %pad_add_fusion.bounds, bf16[256,1024]{1,0:T(8,128)(2,1)S(1)} %copy-done.7, bf16[2,256,128]{2,1,0:T(8,128)(2,1)S(1)} %copy-done.3, bf16[4,16,2,64,128]{4,3,2,1,0:T(8,128)(2,1)S(1)} %bitcast.9, bf16[256,1024]{1,0:T(8,128)(2,1)} %shard_map.102.rest_0_), custom_call_target="tpu_custom_call", output_to_operand_aliasing={{}: (4, {})} | custom-call | flops 2281701376 | bytes 2097152 | tf_op jit(solution)/shard_map/pallas_call | solution.py:69
  (39 shorter events, 6.0 us)
Async XLA Ops:
  8.7 1.0 copy-start.2
  9.7 0.8 copy-start.4
  11.4 30.5 %copy-start.8 = (bf16[2,64,128]{2,1,0:T(8,128)(2,1)S(1)}, bf16[2,64,128]{2,1,0:T(8,128)(2,1)}, u32[]{:S(2)}) copy-start(bf16[2,64,128]{2,1,0:T(8,128)(2,1)} %param.10) | copy-start | bytes 98308
  11.4 25.2 %all-to-all-start = ((bf16[4,512,128]{2,1,0:T(8,128)(2,1)}), bf16[4,512,128]{2,1,0:T(8,128)(2,1)S(1)}, u32[]{:S(2)}, u32[]{:S(2)}) async-start(bf16[4,512,128]{2,1,0:T(8,128)(2,1)} %shard_map.95), calls=%async_computation | async-start | bytes 1048576 | tf_op jit(solution)/shard_map/all_to_all | solution.py:191
  16.5 81.2 %all-gather.4.cloned.1.call-start = ((), (), s32[]{:S(2)}) async-start(), calls=%async_computation.7 | async-start | bytes 2703360 | tf_op jit(solution)/shard_map/all_gather | solution.py:230
  16.5 15.2 %collective-permute-start.2 = (bf16[1,528,128]{2,1,0:T(8,128)(2,1)S(1)}, bf16[1,528,128]{2,1,0:T(8,128)(2,1)S(1)}, u32[]{:S(2)}, u32[]{:S(2)}) collective-permute-start(bf16[1,528,128]{2,1,0:T(8,128)(2,1)S(1)} %bitcast.10), channel_id=1, source_target_pairs={{0,16},{8,24},{16,32},{24,40},{32,48},{40,56},{48,64},{56,72},{64,... | collective-permute-start | bytes 405512 | tf_op jit(solution)/shard_map/ppermute | solution.py:228
  21.4 10.3 %collective-permute-start.1 = (bf16[1,528,128]{2,1,0:T(8,128)(2,1)S(1)}, bf16[1,528,128]{2,1,0:T(8,128)(2,1)S(1)}, u32[]{:S(2)}, u32[]{:S(2)}) collective-permute-start(bf16[1,528,128]{2,1,0:T(8,128)(2,1)S(1)} %bitcast.11), channel_id=1, source_target_pairs={{0,120},{8,0},{16,8},{24,16},{32,24},{40,32},{48,40},{56,48},{64,5... | collective-permute-start | bytes 405512 | tf_op jit(solution)/shard_map/ppermute | solution.py:228
  29.6 7.0 %collective-permute-start = (bf16[1,528,128]{2,1,0:T(8,128)(2,1)S(1)}, bf16[1,528,128]{2,1,0:T(8,128)(2,1)S(1)}, u32[]{:S(2)}, u32[]{:S(2)}) collective-permute-start(bf16[1,528,128]{2,1,0:T(8,128)(2,1)S(1)} %bitcast.12), channel_id=1, source_target_pairs={{0,8},{8,16},{16,24},{24,32},{32,40},{40,48},{48,56},{56,64},{64,7... | collective-permute-start | bytes 405512 | tf_op jit(solution)/shard_map/ppermute | solution.py:228
  38.5 17.3 %all-to-all-start.1 = ((f32[4,64,256]{2,1,0:T(8,128)}), f32[4,64,256]{2,1,0:T(8,128)S(1)}, u32[]{:S(2)}, u32[]{:S(2)}) async-start(f32[4,64,256]{2,1,0:T(8,128)} %shard_map.96), calls=%async_computation.1 | async-start | bytes 524288 | tf_op jit(solution)/shard_map/all_to_all | solution.py:191
  41.9 13.9 %collective-permute-start.3 = (bf16[1,2,64,128]{3,2,1,0:T(8,128)(2,1)S(1)}, bf16[1,2,64,128]{3,2,1,0:T(8,128)(2,1)S(1)}, u32[]{:S(2)}, u32[]{:S(2)}) collective-permute-start(bf16[1,2,64,128]{3,2,1,0:T(8,128)(2,1)S(1)} %bitcast.14), channel_id=1, source_target_pairs={{0,64},{8,72},{16,80},{24,88},{32,96},{40,104},{48,112},{56,120},{... | collective-permute-start | bytes 98312 | tf_op jit(solution)/shard_map/ppermute | solution.py:195
  56.5 29.4 %all-to-all-start.2 = ((f32[4,64,256]{2,1,0:T(8,128)}), f32[4,64,256]{2,1,0:T(8,128)S(1)}, u32[]{:S(2)}, u32[]{:S(2)}) async-start(f32[4,64,256]{2,1,0:T(8,128)} %broadcast_in_dim.10), calls=%async_computation.2 | async-start | bytes 524288 | tf_op jit(solution)/shard_map/all_to_all | solution.py:191
  64.8 82.3 %all-gather.6.cloned.1.call-start = ((), (), s32[]{:S(2)}) async-start(), calls=%async_computation.8 | async-start | bytes 2621440 | tf_op jit(solution)/shard_map/all_gather | solution.py:254
  64.8 12.4 %collective-permute-start.4 = (bf16[2,2,64,128]{3,2,1,0:T(8,128)(2,1)S(1)}, bf16[2,2,64,128]{3,2,1,0:T(8,128)(2,1)S(1)}, u32[]{:S(2)}, u32[]{:S(2)}) collective-permute-start(bf16[2,2,64,128]{3,2,1,0:T(8,128)(2,1)S(1)} %pad_maximum_fusion.4), channel_id=1, source_target_pairs={{0,32},{8,40},{16,48},{24,56},{32,0},{40,8},{48,16},{56,24},{64,96... | collective-permute-start | bytes 196616 | tf_op jit(solution)/shard_map/ppermute | solution.py:195
  77.2 8.7 %collective-permute-start.5 = (bf16[4,2,64,128]{3,2,1,0:T(8,128)(2,1)S(1)}, bf16[4,2,64,128]{3,2,1,0:T(8,128)(2,1)S(1)}, u32[]{:S(2)}, u32[]{:S(2)}) collective-permute-start(bf16[4,2,64,128]{3,2,1,0:T(8,128)(2,1)S(1)} %pad_maximum_fusion.3), channel_id=1, source_target_pairs={{0,16},{8,24},{16,0},{24,8},{32,48},{40,56},{48,32},{56,40},{64,80... | collective-permute-start | bytes 393224 | tf_op jit(solution)/shard_map/ppermute | solution.py:195
  86.0 10.9 %collective-permute-start.6 = (bf16[8,2,64,128]{3,2,1,0:T(8,128)(2,1)S(1)}, bf16[8,2,64,128]{3,2,1,0:T(8,128)(2,1)S(1)}, u32[]{:S(2)}, u32[]{:S(2)}) collective-permute-start(bf16[8,2,64,128]{3,2,1,0:T(8,128)(2,1)S(1)} %pad_maximum_fusion.2), channel_id=1, source_target_pairs={{0,8},{8,0},{16,24},{24,16},{32,40},{40,32},{48,56},{56,48},{64,72... | collective-permute-start | bytes 786440 | tf_op jit(solution)/shard_map/ppermute | solution.py:195
  97.7 1.6 copy-start
  100.9 51.4 %copy-start.3 = (bf16[2,256,128]{2,1,0:T(8,128)(2,1)S(1)}, bf16[2,256,128]{2,1,0:T(8,128)(2,1)}, u32[]{:S(2)}) copy-start(bf16[2,256,128]{2,1,0:T(8,128)(2,1)} %own_ref.7) | copy-start | bytes 393220
  100.9 51.4 %copy-start.7 = (bf16[256,1024]{1,0:T(8,128)(2,1)S(1)}, bf16[256,1024]{1,0:T(8,128)(2,1)}, u32[]{:S(2)}) copy-start(bf16[256,1024]{1,0:T(8,128)(2,1)} %q_ref.9) | copy-start | bytes 1572868
  147.9 10.6 %all-to-all-start.5 = ((bf16[4,4,64,256]{3,2,1,0:T(8,128)(2,1)}), bf16[4,4,64,256]{3,2,1,0:T(8,128)(2,1)S(1)}, u32[]{:S(2)}, u32[]{:S(2)}) async-start(bf16[4,4,64,256]{3,2,1,0:T(8,128)(2,1)} %broadcast_in_dim.11), calls=%async_computation.5 | async-start | bytes 1048576 | tf_op jit(solution)/shard_map/all_to_all | solution.py:191
  152.3 1.6 copy-start.5
  153.9 4.7 %copy-start.1 = (bf16[1024,128]{1,0:T(8,128)(2,1)S(1)}, bf16[1024,128]{1,0:T(8,128)(2,1)}, u32[]{:S(2)}) copy-start(bf16[1024,128]{1,0:T(8,128)(2,1)} %w_ref.3) | copy-start | bytes 786436
  153.9 5.6 %copy-start.6 = (bf16[64,2,64,128]{3,2,1,0:T(8,128)(2,1)S(1)}, bf16[64,2,64,128]{3,2,1,0:T(8,128)(2,1)}, u32[]{:S(2)}) copy-start(bf16[64,2,64,128]{3,2,1,0:T(8,128)(2,1)} %all-gather.6.cloned.1.call-done) | copy-start | bytes 6291460
  168.7 14.4 %all-to-all-start.6 = ((f32[8,32,128]{2,1,0:T(8,128)}), f32[8,32,128]{2,1,0:T(8,128)S(1)}, u32[]{:S(2)}, u32[]{:S(2)}) async-start(f32[8,32,128]{2,1,0:T(8,128)} %shard_map.100), calls=%async_computation.6 | async-start | bytes 262144 | tf_op jit(solution)/shard_map/all_to_all | solution.py:191
Sparse Core Ops, SparseCore 0:
  37.6 39.7 all-gather.3
  101.1 45.9 all-gather.5

commit v2 on v1

--- a/solution.py
+++ b/solution.py
@@ -54,9 +54,9 @@
     out_ref[:, HD:] = mixed[rows:].astype(jnp.bfloat16)
 
 
-def context_attention(queries, own, anchors, bounds, previous, index):
+def context_attention(queries, own, anchors, bounds, previous, index, steps):
     rows, width = queries.shape
-    columns = pl.BlockSpec((rows, 2 * HD), lambda i, b: (0, index))
+    columns = pl.BlockSpec((rows, 2 * HD), lambda i, b: (0, index + i))
     whole = lambda array: pl.BlockSpec(array.shape, lambda i, b: (0,) * array.ndim)
     operands = [queries, own, anchors]
     in_specs = [columns, whole(own), whole(anchors)]
@@ -69,13 +69,15 @@
     return pl.pallas_call(
         context_kernel,
         grid_spec=pltpu.PrefetchScalarGridSpec(
-            num_scalar_prefetch=1, grid=(1,), in_specs=in_specs, out_specs=columns
+            num_scalar_prefetch=1, grid=(steps,), in_specs=in_specs, out_specs=columns
         ),
         out_shape=jax.ShapeDtypeStruct((rows, width), jnp.bfloat16),
         input_output_aliases=aliases,
         compiler_params=pltpu.CompilerParams(vmem_limit_bytes=VMEM_LIMIT),
         cost_estimate=pl.CostEstimate(
-            flops=16 * rows * keys * HD, bytes_accessed=2 * anchors.size, transcendentals=2 * rows * keys
+            flops=16 * steps * rows * keys * HD,
+            bytes_accessed=2 * anchors.size,
+            transcendentals=2 * steps * rows * keys,
         ),
     )(bounds, *operands)
 
@@ -115,9 +117,15 @@
     return jnp.transpose(jnp.broadcast_to(row, (size, size)))
 
 
+def terms(value):
+    high = value.astype(jnp.bfloat16).astype(jnp.float32)
+    middle = (value - high).astype(jnp.bfloat16).astype(jnp.float32)
+    return [high, middle, value - high - middle]
+
+
 def section_kernel(length, q_ref, cache_ref, out_ref):
     heads = q_ref.shape[1] // HD
-    size = out_ref.shape[1] - 8
+    size = out_ref.shape[1] - 16
     queries = jnp.concatenate([q_ref[:, head * HD : (head + 1) * HD] for head in range(heads)], axis=0)
     state = None
     for first in range(0, cache_ref.shape[0], 4):
@@ -132,25 +140,25 @@
     row_max, total, out = state
     row_max = jnp.transpose(jnp.broadcast_to(row_max, (size, HD)))
     total = jnp.transpose(jnp.broadcast_to(total, (size, HD)))
-    stats = jnp.concatenate([row_max[:4], total[:4]], axis=0)
+    stats = jnp.concatenate(terms(row_max[:1]) + terms(total[:1]) + [jnp.zeros((10, size), jnp.float32)], axis=0)
     for copy in range(out_ref.shape[0]):
-        out_ref[copy, :size] = out
-        out_ref[copy, size:] = stats
+        out_ref[copy, :size] = out.astype(jnp.bfloat16)
+        out_ref[copy, size:] = stats.astype(jnp.bfloat16)
 
 
 def finish_kernel(in_ref, out_ref):
     parts = in_ref.shape[0]
-    size = in_ref.shape[1] - 8
+    size = in_ref.shape[1] - 16
     rows = out_ref.shape[1]
-    maxes = [in_ref[part, size : size + 1] for part in range(parts)]
+    stats = [in_ref[part, size:].astype(jnp.float32) for part in range(parts)]
+    maxes = [tile[0:1] + tile[1:2] + tile[2:3] for tile in stats]
     joint = functools.reduce(jnp.maximum, maxes)
     rates = [jnp.exp2((other - joint) * RATE) for other in maxes]
-    total = 0.0
+    total, mixed = 0.0, 0.0
     for part in range(parts):
-        total = total + rates[part] * in_ref[part, size + 4 : size + 5]
-    mixed = 0.0
-    for part in range(parts):
-        mixed = mixed + across(rates[part], size) * in_ref[part, :size]
+        tile = stats[part]
+        total = total + rates[part] * (tile[3:4] + tile[4:5] + tile[5:6])
+        mixed = mixed + across(rates[part], size) * in_ref[part, :size].astype(jnp.float32)
     mixed = (mixed / across(total, size)).astype(jnp.bfloat16)
     for copy in range(out_ref.shape[0]):
         for head in range(size // rows):
@@ -190,10 +198,6 @@
     def swap(array, axis):
         return lax.all_to_all(array, axis, 0, 0, tiled=True)
 
-    def double(block, distance):
-        pairs = [(z, z ^ distance) for z in range(nz)]
-        return jnp.concatenate([block, lax.ppermute(block, ("h", "l"), pairs)], axis=0)
-
     def body(ctx_q, ctx_kv, anchor_kv, counts, offsets, query_in, w_query, w_out):
         rows = ctx_q.shape[0]
         heads = ctx_q.shape[1] // HD
@@ -213,14 +217,11 @@
             )(*operands)
 
         each = nh * share
-        distances = [nz >> (step + 1) for step in range(nz.bit_length() - 1)]
-        anchors = anchor_kv[None]
 
         packed = kernel(pack_kernel, (ny, qrows + part_heads * depth, HD), bf16, query_in, w_query)
         cache = jnp.concatenate(
             [ctx_kv.reshape(2 * rows, HD), jnp.broadcast_to(counts[0].astype(bf16), (16, HD))], axis=0
         )
-        packed, cache = tie((packed, cache))
         packed = swap(packed, "y")
         window = [cache[None]]
         for shift in (1, -1, 2)[: nl - 1]:
@@ -233,20 +234,16 @@
             functools.partial(project_kernel, depth, share), (nl, each, width), f32, packed
         )
         partial = swap(partial, "l")
-        for distance in distances[:-3]:
-            anchors = double(anchors, distance)
-        partial, anchors = tie((partial, anchors))
-        partial = swap(spread(partial.sum(0), nh), "h")
-        for distance in distances[-3:-1]:
-            anchors = double(anchors, distance)
+        partial, anchors = tie((spread(partial.sum(0), nh), anchor_kv[None]))
+        partial = swap(partial, "h")
+        anchors = lax.all_gather(anchors, ("h", "l"), axis=0, tiled=True)
         partial, anchors = tie((partial, anchors))
         projected = partial.sum(0).astype(bf16)
-        anchors = double(anchors, distances[-1])
 
         state = kernel(
             functools.partial(section_kernel, rows),
-            (nh, part_heads * each + 8, HD),
-            f32,
+            (nh, part_heads * each + 16, HD),
+            bf16,
             projected,
             caches,
         )
@@ -257,18 +254,19 @@
         attended = swap(attended, "l")
 
         bounds = jnp.stack([counts[0], offsets[0]])
-        attend = lambda previous, index: context_attention(ctx_q, ctx_kv, anchors, bounds, previous, index)
+        attend = lambda previous, index, steps: context_attention(
+            ctx_q, ctx_kv, anchors, bounds, previous, index, steps
+        )
         attended, anchors = tie((attended, anchors))
         attended = swap(spread(attended, ny), "y")
-        ctx_attn = attend(None, 0)
+        ctx_attn = attend(None, 0, 1)
         attended, ctx_attn = tie((attended, ctx_attn))
         product = kernel(
             functools.partial(output_kernel, share), (nt, qrows // nt, HD), f32, attended, w_out
         )
         product, ctx_attn = tie((product, ctx_attn))
         product = swap(product, tp)
-        for index in range(1, heads // 2):
-            ctx_attn = attend(ctx_attn, index)
+        ctx_attn = attend(ctx_attn, 1, heads // 2 - 1)
         result = product.sum(0).astype(bf16)
         return (ctx_attn, result)
 

time: 191 us -> 180 us (0.942)
  starting transfers between devices: 72 us -> 37.1 us
  blocking collectives: 43.3 us -> 73.4 us
  Pallas kernels: 23 us -> 20 us
  waiting for transfers between devices: 26.8 us -> 24.1 us
    all_gather x0 -> x1, blocking collectives: none -> 36.4 us  [body(): anchors = lax.all_gather(anchors, ('h', 'l'), axis=0, tiled=True)]
    ppermute x4 -> x0, starting transfers between devices: 27.6 us -> none  [double(): lax.ppermute(block, ('h', 'l'), pairs)]
    ppermute x4 -> x0, waiting for transfers between devices: 18.3 us -> none  [double(): lax.ppermute(block, ('h', 'l'), pairs)]
    all_gather x1, waiting for transfers between devices: 2.7 us -> 17.1 us  [body(): anchors = lax.all_gather(anchors, 'y', axis=0, tiled=False)]
    all_to_all x5 -> x4, starting transfers between devices: 29.5 us -> 22.1 us  [swap(): return lax.all_to_all(array, axis, 0, 0, tiled=True)]
    all_to_all x2 -> x3, blocking collectives: 43.3 us -> 37 us  [swap(): return lax.all_to_all(array, axis, 0, 0, tiled=True)]
    pallas_call x4 -> x2, Pallas kernels: 18.5 us -> 16.2 us  [context_attention(): pl.pallas_call(context_kernel, grid_spec=pltpu.PrefetchScalarGridSpec(num...]
  transfers between devices with their start and end apart: 14 -> 9, of which waited for: 8 -> 4; matrix products, arithmetic and copies ran while one was open for 1% -> 1% of each run, Pallas kernels for 5% -> 9%
where the time goes in v2:
time: 180 us; the launch traced here: 179 us
  blocking collectives  73.4 us (41%)
  starting transfers between devices  37.1 us (21%)
  waiting for transfers between devices  24.1 us (13%)
  Pallas kernels  20 us (11%)
  between operations  15.4 us (9%)
  local copies, waits for them, and re-layouts  7.51 us (4%)
    all_to_all x3, blocking collectives, swap(): return lax.all_to_all(array, axis, 0, 0, tiled=True)  37 us
    all_gather x1, blocking collectives, body(): anchors = lax.all_gather(anchors, ('h', 'l'), axis=0, tiled=True)  36.4 us
    all_to_all x4, starting transfers between devices, swap(): return lax.all_to_all(array, axis, 0, 0, tiled=True)  22.1 us
    all_gather x1, waiting for transfers between devices, body(): anchors = lax.all_gather(anchors, 'y', axis=0, tiled=False)  17.1 us
    pallas_call x2, Pallas kernels, context_attention(): pl.pallas_call(context_kernel, grid_spec=pltpu.PrefetchScalarGridSpec(num...  16.2 us
    ppermute x3, starting transfers between devices, body(): window.append(lax.ppermute(cache[None], ('h', 'l'), pairs))  15 us
    ppermute x3, waiting for transfers between devices, body(): window.append(lax.ppermute(cache[None], ('h', 'l'), pairs))  5.04 us
    unnamed x18, local copies, waits for them, and re-layouts  5 us
  transfers between devices with their start and end apart: 9, of which 4 were waited for; matrix products, arithmetic and copies ran while one was open for 1% of the time, Pallas kernels for 9%

profile of v2, /device:TPU:1, one launch (start us, length us, event | category | flops | bytes accessed | tf_op | source)
XLA Modules:
  0.0 179.1 jit_solution(15418643726917509580)
XLA Ops:
  7.2 0.9 copy-done.2
  8.1 0.8 copy-done.4
  9.0 0.9 shard_map.95
  9.8 5.0 %all-to-all-start = ((bf16[4,512,128]{2,1,0:T(8,128)(2,1)}), bf16[4,512,128]{2,1,0:T(8,128)(2,1)S(1)}, u32[]{:S(2)}, u32[]{:S(2)}) async-start(bf16[4,512,128]{2,1,0:T(8,128)(2,1)} %shard_map.95), calls=%async_computation | async-start | bytes 1048576 | tf_op jit(solution)/shard_map/all_to_all | solution.py:199
  15.5 0.9 pad_bitcast_fusion
  16.4 4.9 %collective-permute-start.2 = (bf16[1,528,128]{2,1,0:T(8,128)(2,1)S(1)}, bf16[1,528,128]{2,1,0:T(8,128)(2,1)S(1)}, u32[]{:S(2)}, u32[]{:S(2)}) collective-permute-start(bf16[1,528,128]{2,1,0:T(8,128)(2,1)S(1)} %pad_bitcast_fusion), channel_id=1, source_target_pairs={{0,16},{8,24},{16,32},{24,40},{32,48},{40,56},{48,64},{56,72},{64,... | collective-permute-start | bytes 405512 | tf_op jit(solution)/shard_map/ppermute | solution.py:229
  21.3 8.1 %collective-permute-start.1 = (bf16[1,528,128]{2,1,0:T(8,128)(2,1)S(1)}, bf16[1,528,128]{2,1,0:T(8,128)(2,1)S(1)}, u32[]{:S(2)}, u32[]{:S(2)}) collective-permute-start(bf16[1,528,128]{2,1,0:T(8,128)(2,1)S(1)} %pad_bitcast_fusion), channel_id=1, source_target_pairs={{0,120},{8,0},{16,8},{24,16},{32,24},{40,32},{48,40},{56,48},{64,5... | collective-permute-start | bytes 405512 | tf_op jit(solution)/shard_map/ppermute | solution.py:229
  29.5 1.9 %collective-permute-start = (bf16[1,528,128]{2,1,0:T(8,128)(2,1)S(1)}, bf16[1,528,128]{2,1,0:T(8,128)(2,1)S(1)}, u32[]{:S(2)}, u32[]{:S(2)}) collective-permute-start(bf16[1,528,128]{2,1,0:T(8,128)(2,1)S(1)} %pad_bitcast_fusion), channel_id=1, source_target_pairs={{0,8},{8,16},{16,24},{24,32},{32,40},{40,48},{48,56},{56,64},{64,7... | collective-permute-start | bytes 405512 | tf_op jit(solution)/shard_map/ppermute | solution.py:229
  31.4 0.2 collective-permute-done.2
  31.6 4.8 %collective-permute-done = bf16[1,528,128]{2,1,0:T(8,128)(2,1)S(1)} collective-permute-done((bf16[1,528,128]{2,1,0:T(8,128)(2,1)S(1)}, bf16[1,528,128]{2,1,0:T(8,128)(2,1)S(1)}, u32[]{:S(2)}, u32[]{:S(2)}) %collective-permute-start) | collective-permute-done | bytes 135200 | tf_op jit(solution)/shard_map/ppermute | solution.py:229
  36.5 0.9 pad_maximum_fusion
  37.3 0.3 shard_map.96
  37.6 9.2 %all_to_all.35 = f32[4,64,256]{2,1,0:T(8,128)S(1)} all-to-all(f32[4,64,256]{2,1,0:T(8,128)S(1)} %shard_map.96), channel_id=1, replica_groups=mesh['y'=4,'h'=4,'l'=4,'x'=4,'c'=2] {'l'}, dimensions={0} | all-to-all | bytes 524288 | tf_op jit(solution)/shard_map/all_to_all | solution.py:199
  46.9 0.7 broadcast_in_dim.9
  47.6 7.8 %all-to-all-start.2 = ((f32[4,64,256]{2,1,0:T(8,128)}), f32[4,64,256]{2,1,0:T(8,128)S(1)}, u32[]{:S(2)}, u32[]{:S(2)}) async-start(f32[4,64,256]{2,1,0:T(8,128)} %broadcast_in_dim.9), calls=%async_computation.2 | async-start | bytes 524288 | tf_op jit(solution)/shard_map/all_to_all | solution.py:199
  55.5 36.4 %all_gather.12 = bf16[16,2,64,128]{3,2,1,0:T(8,128)(2,1)} all-gather(bf16[1,2,64,128]{3,2,1,0:T(8,128)(2,1)S(1)} %bitcast.9), channel_id=1, replica_groups=mesh['y'=4,'h'=4,'l'=4,'x'=4,'c'=2] {'h','l'}, dimensions={0}, use_global_device_ids=true | all-gather | bytes 557056 | tf_op jit(solution)/shard_map/all_gather | solution.py:239
  91.9 1.6 copy-done
  93.5 1.6 shard_map.97
  95.1 19.8 %all_to_all.36.in_ref = bf16[4,144,128]{2,1,0:T(8,128)(2,1)S(1)} all-to-all(bf16[4,144,128]{2,1,0:T(8,128)(2,1)S(1)} %shard_map.97), channel_id=1, replica_groups=mesh['y'=4,'h'=4,'l'=4,'x'=4,'c'=2] {'h'}, dimensions={0} | all-to-all | bytes 294912 | tf_op jit(solution)/shard_map/all_to_all | solution.py:199
  114.9 0.2 shard_map.98
  115.1 8.0 %all_to_all.37 = bf16[4,64,256]{2,1,0:T(8,128)(2,1)S(1)} all-to-all(bf16[4,64,256]{2,1,0:T(8,128)(2,1)S(1)} %shard_map.98), channel_id=1, replica_groups=mesh['y'=4,'h'=4,'l'=4,'x'=4,'c'=2] {'l'}, dimensions={0} | all-to-all | bytes 262144 | tf_op jit(solution)/shard_map/all_to_all | solution.py:199
  123.1 17.1 %all-gather.6.cloned.1.call-done = bf16[64,2,64,128]{3,2,1,0:T(8,128)(2,1)} async-done(((bf16[16,2,64,128]{3,2,1,0:T(8,128)(2,1)}), bf16[64,2,64,128]{3,2,1,0:T(8,128)(2,1)}) %all-gather.6.cloned.1.call-update) | async-done | bytes 2097168 | tf_op jit(solution)/shard_map/all_gather | solution.py:251
  140.2 0.9 broadcast_in_dim.11
  141.0 3.5 %all-to-all-start.5 = ((bf16[4,4,64,256]{3,2,1,0:T(8,128)(2,1)}), bf16[4,4,64,256]{3,2,1,0:T(8,128)(2,1)S(1)}, u32[]{:S(2)}, u32[]{:S(2)}) async-start(bf16[4,4,64,256]{3,2,1,0:T(8,128)(2,1)} %broadcast_in_dim.11), calls=%async_computation.5 | async-start | bytes 1048576 | tf_op jit(solution)/shard_map/all_to_all | solution.py:199
  145.2 0.1 pad_add_fusion.bounds
  145.3 1.6 copy-done.5
  146.8 4.6 %shard_map.99.rest_0_ = bf16[256,1024]{1,0:T(8,128)(2,1)} custom-call(s32[2]{0:T(128)S(1)} %pad_add_fusion.bounds, bf16[256,1024]{1,0:T(8,128)(2,1)S(1)} %copy-done.7, bf16[2,256,128]{2,1,0:T(8,128)(2,1)S(1)} %copy-done.3, bf16[4,16,2,64,128]{4,3,2,1,0:T(8,128)(2,1)S(1)} %bitcast.7), custom_call_target="tpu_custom_call" | custom-call | flops 2281701376 | bytes 2097152 | tf_op jit(solution)/shard_map/pallas_call | solution.py:69
  151.5 1.9 %all-to-all-done.5.att_ref = bf16[4,4,64,256]{3,2,1,0:T(8,128)(2,1)S(1)} async-done(((bf16[4,4,64,256]{3,2,1,0:T(8,128)(2,1)}), bf16[4,4,64,256]{3,2,1,0:T(8,128)(2,1)S(1)}, u32[]{:S(2)}, u32[]{:S(2)}) %all-to-all-start.5) | async-done | bytes 524320 | tf_op jit(solution)/shard_map/all_to_all | solution.py:199
  153.4 0.9 shard_map.100
  154.3 5.8 %all-to-all-start.6 = ((f32[8,32,128]{2,1,0:T(8,128)}), f32[8,32,128]{2,1,0:T(8,128)S(1)}, u32[]{:S(2)}, u32[]{:S(2)}) async-start(f32[8,32,128]{2,1,0:T(8,128)} %shard_map.100), calls=%async_computation.6 | async-start | bytes 262144 | tf_op jit(solution)/shard_map/all_to_all | solution.py:199
  160.1 11.6 %shard_map.101 = bf16[256,1024]{1,0:T(8,128)(2,1)} custom-call(s32[2]{0:T(128)S(1)} %pad_add_fusion.bounds, bf16[256,1024]{1,0:T(8,128)(2,1)S(1)} %copy-done.7, bf16[2,256,128]{2,1,0:T(8,128)(2,1)S(1)} %copy-done.3, bf16[4,16,2,64,128]{4,3,2,1,0:T(8,128)(2,1)S(1)} %bitcast.8, bf16[256,1024]{1,0:T(8,128)(2,1)} %shard_map.99.rest_0_), custom_call_target="tpu_custom_call", output_to_operand_aliasing={{}: (4, {})} | custom-call | flops 6845104128 | bytes 2097152 | tf_op jit(solution)/shard_map/pallas_call | solution.py:69
  171.7 0.6 reduce_sum.29
  (25 shorter events, 0.1 us)
Async XLA Ops:
  7.2 1.0 copy-start.2
  8.1 0.8 copy-start.4
  9.8 26.6 %all-to-all-start = ((bf16[4,512,128]{2,1,0:T(8,128)(2,1)}), bf16[4,512,128]{2,1,0:T(8,128)(2,1)S(1)}, u32[]{:S(2)}, u32[]{:S(2)}) async-start(bf16[4,512,128]{2,1,0:T(8,128)(2,1)} %shard_map.95), calls=%async_computation | async-start | bytes 1048576 | tf_op jit(solution)/shard_map/all_to_all | solution.py:199
  14.8 77.1 %all-gather.4.cloned.1.call-start = ((), (), s32[]{:S(2)}) async-start(), calls=%async_computation.7 | async-start | bytes 2703360 | tf_op jit(solution)/shard_map/all_gather | solution.py:231
  15.5 40.0 %copy-start.8 = (bf16[2,64,128]{2,1,0:T(8,128)(2,1)S(1)}, bf16[2,64,128]{2,1,0:T(8,128)(2,1)}, u32[]{:S(2)}) copy-start(bf16[2,64,128]{2,1,0:T(8,128)(2,1)} %param.10) | copy-start | bytes 98308
  16.4 15.2 %collective-permute-start.2 = (bf16[1,528,128]{2,1,0:T(8,128)(2,1)S(1)}, bf16[1,528,128]{2,1,0:T(8,128)(2,1)S(1)}, u32[]{:S(2)}, u32[]{:S(2)}) collective-permute-start(bf16[1,528,128]{2,1,0:T(8,128)(2,1)S(1)} %pad_bitcast_fusion), channel_id=1, source_target_pairs={{0,16},{8,24},{16,32},{24,40},{32,48},{40,56},{48,64},{56,72},{64,... | collective-permute-start | bytes 405512 | tf_op jit(solution)/shard_map/ppermute | solution.py:229
  21.3 10.3 %collective-permute-start.1 = (bf16[1,528,128]{2,1,0:T(8,128)(2,1)S(1)}, bf16[1,528,128]{2,1,0:T(8,128)(2,1)S(1)}, u32[]{:S(2)}, u32[]{:S(2)}) collective-permute-start(bf16[1,528,128]{2,1,0:T(8,128)(2,1)S(1)} %pad_bitcast_fusion), channel_id=1, source_target_pairs={{0,120},{8,0},{16,8},{24,16},{32,24},{40,32},{48,40},{56,48},{64,5... | collective-permute-start | bytes 405512 | tf_op jit(solution)/shard_map/ppermute | solution.py:229
  29.5 7.0 %collective-permute-start = (bf16[1,528,128]{2,1,0:T(8,128)(2,1)S(1)}, bf16[1,528,128]{2,1,0:T(8,128)(2,1)S(1)}, u32[]{:S(2)}, u32[]{:S(2)}) collective-permute-start(bf16[1,528,128]{2,1,0:T(8,128)(2,1)S(1)} %pad_bitcast_fusion), channel_id=1, source_target_pairs={{0,8},{8,16},{16,24},{24,32},{32,40},{40,48},{48,56},{56,64},{64,7... | collective-permute-start | bytes 405512 | tf_op jit(solution)/shard_map/ppermute | solution.py:229
  47.6 44.2 %all-to-all-start.2 = ((f32[4,64,256]{2,1,0:T(8,128)}), f32[4,64,256]{2,1,0:T(8,128)S(1)}, u32[]{:S(2)}, u32[]{:S(2)}) async-start(f32[4,64,256]{2,1,0:T(8,128)} %broadcast_in_dim.9), calls=%async_computation.2 | async-start | bytes 524288 | tf_op jit(solution)/shard_map/all_to_all | solution.py:199
  55.5 84.7 %all-gather.6.cloned.1.call-start = ((), (), s32[]{:S(2)}) async-start(), calls=%async_computation.8 | async-start | bytes 2621440 | tf_op jit(solution)/shard_map/all_gather | solution.py:251
  91.9 1.6 copy-start
  93.5 51.7 %copy-start.3 = (bf16[2,256,128]{2,1,0:T(8,128)(2,1)S(1)}, bf16[2,256,128]{2,1,0:T(8,128)(2,1)}, u32[]{:S(2)}) copy-start(bf16[2,256,128]{2,1,0:T(8,128)(2,1)} %own_ref.3) | copy-start | bytes 393220
  93.5 51.7 %copy-start.7 = (bf16[256,1024]{1,0:T(8,128)(2,1)S(1)}, bf16[256,1024]{1,0:T(8,128)(2,1)}, u32[]{:S(2)}) copy-start(bf16[256,1024]{1,0:T(8,128)(2,1)} %q_ref.5) | copy-start | bytes 1572868
  141.0 12.3 %all-to-all-start.5 = ((bf16[4,4,64,256]{3,2,1,0:T(8,128)(2,1)}), bf16[4,4,64,256]{3,2,1,0:T(8,128)(2,1)S(1)}, u32[]{:S(2)}, u32[]{:S(2)}) async-start(bf16[4,4,64,256]{3,2,1,0:T(8,128)(2,1)} %broadcast_in_dim.11), calls=%async_computation.5 | async-start | bytes 1048576 | tf_op jit(solution)/shard_map/all_to_all | solution.py:199
  145.3 1.6 copy-start.5
  146.8 6.5 %copy-start.1 = (bf16[1024,128]{1,0:T(8,128)(2,1)S(1)}, bf16[1024,128]{1,0:T(8,128)(2,1)}, u32[]{:S(2)}) copy-start(bf16[1024,128]{1,0:T(8,128)(2,1)} %w_ref.3) | copy-start | bytes 786436
  146.8 13.3 %copy-start.6 = (bf16[64,2,64,128]{3,2,1,0:T(8,128)(2,1)S(1)}, bf16[64,2,64,128]{3,2,1,0:T(8,128)(2,1)}, u32[]{:S(2)}) copy-start(bf16[64,2,64,128]{3,2,1,0:T(8,128)(2,1)} %all-gather.6.cloned.1.call-done) | copy-start | bytes 6291460
  154.3 17.4 %all-to-all-start.6 = ((f32[8,32,128]{2,1,0:T(8,128)}), f32[8,32,128]{2,1,0:T(8,128)S(1)}, u32[]{:S(2)}, u32[]{:S(2)}) async-start(f32[8,32,128]{2,1,0:T(8,128)} %shard_map.100), calls=%async_computation.6 | async-start | bytes 262144 | tf_op jit(solution)/shard_map/all_to_all | solution.py:199
Sparse Core Ops, SparseCore 0:
  37.5 39.7 all-gather.3
  95.2 44.8 all-gather.5

commit v3 on v2

--- a/solution.py
+++ b/solution.py
@@ -227,17 +227,17 @@
         for shift in (1, -1, 2)[: nl - 1]:
             pairs = [(z, (z + shift) % nz) for z in range(nz)]
             window.append(lax.ppermute(cache[None], ("h", "l"), pairs))
-        packed, window = tie((packed, window))
-        caches = lax.all_gather(jnp.concatenate(window, axis=0), "y", axis=0, tiled=True)
+        window, anchors = tie((jnp.concatenate(window, axis=0), anchor_kv[None]))
+        caches = lax.all_gather(window, "y", axis=0, tiled=True)
+        anchors = lax.all_gather(anchors, ("h", "l"), axis=0, tiled=True)
+        packed, anchors = tie((packed, anchors))
+        anchors = lax.all_gather(anchors, "y", axis=0, tiled=False)
 
         partial = kernel(
             functools.partial(project_kernel, depth, share), (nl, each, width), f32, packed
         )
         partial = swap(partial, "l")
-        partial, anchors = tie((spread(partial.sum(0), nh), anchor_kv[None]))
-        partial = swap(partial, "h")
-        anchors = lax.all_gather(anchors, ("h", "l"), axis=0, tiled=True)
-        partial, anchors = tie((partial, anchors))
+        partial = swap(spread(partial.sum(0), nh), "h")
         projected = partial.sum(0).astype(bf16)
 
         state = kernel(
@@ -247,26 +247,26 @@
             projected,
             caches,
         )
-        state, anchors = tie((state, anchors))
-        anchors = lax.all_gather(anchors, "y", axis=0, tiled=False)
         state = swap(state, "h")
         attended = kernel(finish_kernel, (nl, each, width), bf16, state)
-        attended = swap(attended, "l")
 
         bounds = jnp.stack([counts[0], offsets[0]])
         attend = lambda previous, index, steps: context_attention(
             ctx_q, ctx_kv, anchors, bounds, previous, index, steps
         )
         attended, anchors = tie((attended, anchors))
+        attended = swap(attended, "l")
+        ctx_attn = attend(None, 0, 1)
+        attended, ctx_attn = tie((attended, ctx_attn))
         attended = swap(spread(attended, ny), "y")
-        ctx_attn = attend(None, 0, 1)
+        ctx_attn = attend(ctx_attn, 1, 1)
         attended, ctx_attn = tie((attended, ctx_attn))
         product = kernel(
             functools.partial(output_kernel, share), (nt, qrows // nt, HD), f32, attended, w_out
         )
         product, ctx_attn = tie((product, ctx_attn))
         product = swap(product, tp)
-        ctx_attn = attend(ctx_attn, 1, heads // 2 - 1)
+        ctx_attn = attend(ctx_attn, 2, heads // 2 - 2)
         result = product.sum(0).astype(bf16)
         return (ctx_attn, result)
 

time: 180 us -> 178 us (0.989)
  waiting for transfers between devices: 24.1 us -> 11.4 us
  starting transfers between devices: 37.1 us -> 47 us
  Pallas kernels: 20 us -> 21.9 us
    all_gather x1, waiting for transfers between devices: 17.1 us -> 0.01 us  [body(): anchors = lax.all_gather(anchors, 'y', axis=0, tiled=False)]
    all_to_all x4, starting transfers between devices: 22.1 us -> 31.2 us  [swap(): return lax.all_to_all(array, axis, 0, 0, tiled=True)]
    all_gather x1, blocking collectives: 36.4 us -> 27.4 us  [body(): anchors = lax.all_gather(anchors, ('h', 'l'), axis=0, tiled=True)]
    all_to_all x3, blocking collectives: 37 us -> 45.5 us  [swap(): return lax.all_to_all(array, axis, 0, 0, tiled=True)]
    ppermute x3, waiting for transfers between devices: 5.04 us -> 8.89 us  [body(): window.append(lax.ppermute(cache[None], ('h', 'l'), pairs))]
    pallas_call x2 -> x3, Pallas kernels: 16.2 us -> 17.4 us  [context_attention(): pl.pallas_call(context_kernel, grid_spec=pltpu.PrefetchScalarGridSpec(num...]
  transfers between devices with their start and end apart: 9 -> 9, of which waited for: 4 -> 3; matrix products, arithmetic and copies ran while one was open for 1% -> 0% of each run, Pallas kernels for 9% -> 12%
where the time goes in v3:
time: 178 us; the launch traced here: 177 us
  blocking collectives  72.9 us (41%)
  starting transfers between devices  47 us (26%)
  Pallas kernels  21.9 us (12%)
  between operations  15.5 us (9%)
  waiting for transfers between devices  11.4 us (6%)
  local copies, waits for them, and re-layouts  6.79 us (4%)
    all_to_all x3, blocking collectives, swap(): return lax.all_to_all(array, axis, 0, 0, tiled=True)  45.5 us
    all_to_all x4, starting transfers between devices, swap(): return lax.all_to_all(array, axis, 0, 0, tiled=True)  31.2 us
    all_gather x1, blocking collectives, body(): anchors = lax.all_gather(anchors, ('h', 'l'), axis=0, tiled=True)  27.4 us
    pallas_call x3, Pallas kernels, context_attention(): pl.pallas_call(context_kernel, grid_spec=pltpu.PrefetchScalarGridSpec(num...  17.4 us
    ppermute x3, starting transfers between devices, body(): window.append(lax.ppermute(cache[None], ('h', 'l'), pairs))  15.8 us
    ppermute x3, waiting for transfers between devices, body(): window.append(lax.ppermute(cache[None], ('h', 'l'), pairs))  8.89 us
    unnamed x18, local copies, waits for them, and re-layouts  5.01 us
    pallas_call x5, Pallas kernels, kernel(): pl.pallas_call(body, out_shape=jax.ShapeDtypeStruct(shape, dtype), compil...  4.47 us
  transfers between devices with their start and end apart: 9, of which 3 were waited for; matrix products, arithmetic and copies ran while one was open for 0% of the time, Pallas kernels for 12%

profile of v3, /device:TPU:1, one launch (start us, length us, event | category | flops | bytes accessed | tf_op | source)
XLA Modules:
  0.0 177.1 jit_solution(1082490454774360215)
XLA Ops:
  7.2 0.0 all-gather.4.cloned.1.call-start
  7.9 0.9 pad_bitcast_fusion
  8.8 4.4 %collective-permute-start = (bf16[1,528,128]{2,1,0:T(8,128)(2,1)S(1)}, bf16[1,528,128]{2,1,0:T(8,128)(2,1)S(1)}, u32[]{:S(2)}, u32[]{:S(2)}) collective-permute-start(bf16[1,528,128]{2,1,0:T(8,128)(2,1)S(1)} %pad_bitcast_fusion), channel_id=1, source_target_pairs={{0,8},{8,16},{16,24},{24,32},{32,40},{40,48},{48,56},{56,64},{64,7... | collective-permute-start | bytes 405512 | tf_op jit(solution)/shard_map/ppermute | solution.py:229
  13.2 9.5 %collective-permute-start.1 = (bf16[1,528,128]{2,1,0:T(8,128)(2,1)S(1)}, bf16[1,528,128]{2,1,0:T(8,128)(2,1)S(1)}, u32[]{:S(2)}, u32[]{:S(2)}) collective-permute-start(bf16[1,528,128]{2,1,0:T(8,128)(2,1)S(1)} %pad_bitcast_fusion), channel_id=1, source_target_pairs={{0,120},{8,0},{16,8},{24,16},{32,24},{40,32},{48,40},{56,48},{64,5... | collective-permute-start | bytes 405512 | tf_op jit(solution)/shard_map/ppermute | solution.py:229
  22.7 1.9 %collective-permute-start.2 = (bf16[1,528,128]{2,1,0:T(8,128)(2,1)S(1)}, bf16[1,528,128]{2,1,0:T(8,128)(2,1)S(1)}, u32[]{:S(2)}, u32[]{:S(2)}) collective-permute-start(bf16[1,528,128]{2,1,0:T(8,128)(2,1)S(1)} %pad_bitcast_fusion), channel_id=1, source_target_pairs={{0,16},{8,24},{16,32},{24,40},{32,48},{40,56},{48,64},{56,72},{64,... | collective-permute-start | bytes 405512 | tf_op jit(solution)/shard_map/ppermute | solution.py:229
  24.6 0.3 collective-permute-done.1
  24.9 8.6 %collective-permute-done.2 = bf16[1,528,128]{2,1,0:T(8,128)(2,1)S(1)} collective-permute-done((bf16[1,528,128]{2,1,0:T(8,128)(2,1)S(1)}, bf16[1,528,128]{2,1,0:T(8,128)(2,1)S(1)}, u32[]{:S(2)}, u32[]{:S(2)}) %collective-permute-start.2) | collective-permute-done | bytes 135200 | tf_op jit(solution)/shard_map/ppermute | solution.py:229
  33.5 0.9 pad_maximum_fusion
  34.4 0.9 copy-done.2
  35.4 0.8 copy-done.4
  36.2 0.9 shard_map.95
  37.1 4.2 %all-to-all-start = ((bf16[4,512,128]{2,1,0:T(8,128)(2,1)}), bf16[4,512,128]{2,1,0:T(8,128)(2,1)S(1)}, u32[]{:S(2)}, u32[]{:S(2)}) async-start(bf16[4,512,128]{2,1,0:T(8,128)(2,1)} %shard_map.95), calls=%async_computation | async-start | bytes 1048576 | tf_op jit(solution)/shard_map/all_to_all | solution.py:199
  41.3 27.4 %all_gather.12 = bf16[16,2,64,128]{3,2,1,0:T(8,128)(2,1)} all-gather(bf16[1,2,64,128]{3,2,1,0:T(8,128)(2,1)S(1)} %bitcast.10), channel_id=1, replica_groups=mesh['y'=4,'h'=4,'l'=4,'x'=4,'c'=2] {'h','l'}, dimensions={0}, use_global_device_ids=true | all-gather | bytes 557056 | tf_op jit(solution)/shard_map/all_gather | solution.py:232
  68.7 0.3 shard_map.96
  69.0 8.4 %all_to_all.35 = f32[4,64,256]{2,1,0:T(8,128)S(1)} all-to-all(f32[4,64,256]{2,1,0:T(8,128)S(1)} %shard_map.96), channel_id=1, replica_groups=mesh['y'=4,'h'=4,'l'=4,'x'=4,'c'=2] {'l'}, dimensions={0} | all-to-all | bytes 524288 | tf_op jit(solution)/shard_map/all_to_all | solution.py:199
  77.4 20.3 %all_to_all.36 = f32[4,64,256]{2,1,0:T(8,128)S(1)} all-to-all(f32[4,64,256]{2,1,0:T(8,128)S(1)} %broadcast_in_dim.10), channel_id=1, replica_groups=mesh['y'=4,'h'=4,'l'=4,'x'=4,'c'=2] {'h'}, dimensions={0} | all-to-all | bytes 524288 | tf_op jit(solution)/shard_map/all_to_all | solution.py:199
  97.8 1.6 copy-done
  99.4 1.5 shard_map.97
  100.9 16.8 %all_to_all.37.in_ref = bf16[4,144,128]{2,1,0:T(8,128)(2,1)S(1)} all-to-all(bf16[4,144,128]{2,1,0:T(8,128)(2,1)S(1)} %shard_map.97), channel_id=1, replica_groups=mesh['y'=4,'h'=4,'l'=4,'x'=4,'c'=2] {'h'}, dimensions={0} | all-to-all | bytes 294912 | tf_op jit(solution)/shard_map/all_to_all | solution.py:199
  117.8 0.8 shard_map.98
  118.6 3.9 %all-to-all-start.4 = ((bf16[4,64,256]{2,1,0:T(8,128)(2,1)}), bf16[4,64,256]{2,1,0:T(8,128)(2,1)S(1)}, u32[]{:S(2)}, u32[]{:S(2)}) async-start(bf16[4,64,256]{2,1,0:T(8,128)(2,1)} %shard_map.98), calls=%async_computation.4 | async-start | bytes 262144 | tf_op jit(solution)/shard_map/all_to_all | solution.py:199
  123.2 0.1 pad_add_fusion.bounds
  123.3 1.6 copy-done.5
  124.9 4.6 %shard_map.99.rest_0_ = bf16[256,1024]{1,0:T(8,128)(2,1)} custom-call(s32[2]{0:T(128)S(1)} %pad_add_fusion.bounds, bf16[256,1024]{1,0:T(8,128)(2,1)S(1)} %copy-done.7, bf16[2,256,128]{2,1,0:T(8,128)(2,1)S(1)} %copy-done.3, bf16[4,16,2,64,128]{4,3,2,1,0:T(8,128)(2,1)S(1)} %bitcast.7), custom_call_target="tpu_custom_call" | custom-call | flops 2281701376 | bytes 2097152 | tf_op jit(solution)/shard_map/pallas_call | solution.py:69
  129.5 0.8 broadcast_in_dim.11
  130.3 3.8 %all-to-all-start.5 = ((bf16[4,4,64,256]{3,2,1,0:T(8,128)(2,1)}), bf16[4,4,64,256]{3,2,1,0:T(8,128)(2,1)S(1)}, u32[]{:S(2)}, u32[]{:S(2)}) async-start(bf16[4,4,64,256]{3,2,1,0:T(8,128)(2,1)} %broadcast_in_dim.11), calls=%async_computation.5 | async-start | bytes 1048576 | tf_op jit(solution)/shard_map/all_to_all | solution.py:199
  134.1 4.7 %shard_map.100.rest_0_ = bf16[256,1024]{1,0:T(8,128)(2,1)} custom-call(s32[2]{0:T(128)S(1)} %pad_add_fusion.bounds, bf16[256,1024]{1,0:T(8,128)(2,1)S(1)} %copy-done.7, bf16[2,256,128]{2,1,0:T(8,128)(2,1)S(1)} %copy-done.3, bf16[4,16,2,64,128]{4,3,2,1,0:T(8,128)(2,1)S(1)} %bitcast.8, bf16[256,1024]{1,0:T(8,128)(2,1)} %shard_map.99.rest_0_), custom_call_target="tpu_custom_call", output_to_operand_aliasing={{}: (4, {})} | custom-call | flops 2281701376 | bytes 2097152 | tf_op jit(solution)/shard_map/pallas_call | solution.py:69
  138.8 2.4 %all-to-all-done.5.att_ref = bf16[4,4,64,256]{3,2,1,0:T(8,128)(2,1)S(1)} async-done(((bf16[4,4,64,256]{3,2,1,0:T(8,128)(2,1)}), bf16[4,4,64,256]{3,2,1,0:T(8,128)(2,1)S(1)}, u32[]{:S(2)}, u32[]{:S(2)}) %all-to-all-start.5) | async-done | bytes 524320 | tf_op jit(solution)/shard_map/all_to_all | solution.py:199
  141.2 0.9 shard_map.101
  142.1 19.3 %all-to-all-start.6 = ((f32[8,32,128]{2,1,0:T(8,128)}), f32[8,32,128]{2,1,0:T(8,128)S(1)}, u32[]{:S(2)}, u32[]{:S(2)}) async-start(f32[8,32,128]{2,1,0:T(8,128)} %shard_map.101), calls=%async_computation.6 | async-start | bytes 262144 | tf_op jit(solution)/shard_map/all_to_all | solution.py:199
  161.5 8.2 %shard_map.102 = bf16[256,1024]{1,0:T(8,128)(2,1)} custom-call(s32[2]{0:T(128)S(1)} %pad_add_fusion.bounds, bf16[256,1024]{1,0:T(8,128)(2,1)S(1)} %copy-done.7, bf16[2,256,128]{2,1,0:T(8,128)(2,1)S(1)} %copy-done.3, bf16[4,16,2,64,128]{4,3,2,1,0:T(8,128)(2,1)S(1)} %bitcast.9, bf16[256,1024]{1,0:T(8,128)(2,1)} %shard_map.100.rest_0_), custom_call_target="tpu_custom_call", output_to_operand_aliasing={{}: (4, {})} | custom-call | flops 4563402752 | bytes 2097152 | tf_op jit(solution)/shard_map/pallas_call | solution.py:69
  169.6 0.6 reduce_sum.29
  (26 shorter events, 0.2 us)
Async XLA Ops:
  7.2 34.1 %copy-start.8 = (bf16[2,64,128]{2,1,0:T(8,128)(2,1)S(1)}, bf16[2,64,128]{2,1,0:T(8,128)(2,1)}, u32[]{:S(2)}) copy-start(bf16[2,64,128]{2,1,0:T(8,128)(2,1)} %param.10) | copy-start | bytes 98308
  7.2 90.6 %all-gather.4.cloned.1.call-start = ((), (), s32[]{:S(2)}) async-start(), calls=%async_computation.7 | async-start | bytes 2703360 | tf_op jit(solution)/shard_map/all_gather | solution.py:231
  8.8 15.8 %collective-permute-start = (bf16[1,528,128]{2,1,0:T(8,128)(2,1)S(1)}, bf16[1,528,128]{2,1,0:T(8,128)(2,1)S(1)}, u32[]{:S(2)}, u32[]{:S(2)}) collective-permute-start(bf16[1,528,128]{2,1,0:T(8,128)(2,1)S(1)} %pad_bitcast_fusion), channel_id=1, source_target_pairs={{0,8},{8,16},{16,24},{24,32},{32,40},{40,48},{48,56},{56,64},{64,7... | collective-permute-start | bytes 405512 | tf_op jit(solution)/shard_map/ppermute | solution.py:229
  13.2 11.7 %collective-permute-start.1 = (bf16[1,528,128]{2,1,0:T(8,128)(2,1)S(1)}, bf16[1,528,128]{2,1,0:T(8,128)(2,1)S(1)}, u32[]{:S(2)}, u32[]{:S(2)}) collective-permute-start(bf16[1,528,128]{2,1,0:T(8,128)(2,1)S(1)} %pad_bitcast_fusion), channel_id=1, source_target_pairs={{0,120},{8,0},{16,8},{24,16},{32,24},{40,32},{48,40},{56,48},{64,5... | collective-permute-start | bytes 405512 | tf_op jit(solution)/shard_map/ppermute | solution.py:229
  22.7 10.8 %collective-permute-start.2 = (bf16[1,528,128]{2,1,0:T(8,128)(2,1)S(1)}, bf16[1,528,128]{2,1,0:T(8,128)(2,1)S(1)}, u32[]{:S(2)}, u32[]{:S(2)}) collective-permute-start(bf16[1,528,128]{2,1,0:T(8,128)(2,1)S(1)} %pad_bitcast_fusion), channel_id=1, source_target_pairs={{0,16},{8,24},{16,32},{24,40},{32,48},{40,56},{48,64},{56,72},{64,... | collective-permute-start | bytes 405512 | tf_op jit(solution)/shard_map/ppermute | solution.py:229
  34.4 1.0 copy-start.2
  35.4 0.8 copy-start.4
  37.1 31.6 %all-to-all-start = ((bf16[4,512,128]{2,1,0:T(8,128)(2,1)}), bf16[4,512,128]{2,1,0:T(8,128)(2,1)S(1)}, u32[]{:S(2)}, u32[]{:S(2)}) async-start(bf16[4,512,128]{2,1,0:T(8,128)(2,1)} %shard_map.95), calls=%async_computation | async-start | bytes 1048576 | tf_op jit(solution)/shard_map/all_to_all | solution.py:199
  41.3 77.4 %all-gather.6.cloned.1.call-start = ((), (), s32[]{:S(2)}) async-start(), calls=%async_computation.8 | async-start | bytes 2621440 | tf_op jit(solution)/shard_map/all_gather | solution.py:234
  77.3 45.9 %copy-start.3 = (bf16[2,256,128]{2,1,0:T(8,128)(2,1)S(1)}, bf16[2,256,128]{2,1,0:T(8,128)(2,1)}, u32[]{:S(2)}) copy-start(bf16[2,256,128]{2,1,0:T(8,128)(2,1)} %own_ref.5) | copy-start | bytes 393220
  77.3 45.9 %copy-start.7 = (bf16[256,1024]{1,0:T(8,128)(2,1)S(1)}, bf16[256,1024]{1,0:T(8,128)(2,1)}, u32[]{:S(2)}) copy-start(bf16[256,1024]{1,0:T(8,128)(2,1)} %q_ref.7) | copy-start | bytes 1572868
  97.8 1.6 copy-start
  118.6 10.8 %all-to-all-start.4 = ((bf16[4,64,256]{2,1,0:T(8,128)(2,1)}), bf16[4,64,256]{2,1,0:T(8,128)(2,1)S(1)}, u32[]{:S(2)}, u32[]{:S(2)}) async-start(bf16[4,64,256]{2,1,0:T(8,128)(2,1)} %shard_map.98), calls=%async_computation.4 | async-start | bytes 262144 | tf_op jit(solution)/shard_map/all_to_all | solution.py:199
  123.3 1.6 copy-start.5
  124.8 9.3 %copy-start.6 = (bf16[64,2,64,128]{3,2,1,0:T(8,128)(2,1)S(1)}, bf16[64,2,64,128]{3,2,1,0:T(8,128)(2,1)}, u32[]{:S(2)}) copy-start(bf16[64,2,64,128]{3,2,1,0:T(8,128)(2,1)} %all-gather.6.cloned.1.call-done) | copy-start | bytes 6291460
  130.3 10.9 %all-to-all-start.5 = ((bf16[4,4,64,256]{3,2,1,0:T(8,128)(2,1)}), bf16[4,4,64,256]{3,2,1,0:T(8,128)(2,1)S(1)}, u32[]{:S(2)}, u32[]{:S(2)}) async-start(bf16[4,4,64,256]{3,2,1,0:T(8,128)(2,1)} %broadcast_in_dim.11), calls=%async_computation.5 | async-start | bytes 1048576 | tf_op jit(solution)/shard_map/all_to_all | solution.py:199
  134.1 7.1 %copy-start.1 = (bf16[1024,128]{1,0:T(8,128)(2,1)S(1)}, bf16[1024,128]{1,0:T(8,128)(2,1)}, u32[]{:S(2)}) copy-start(bf16[1024,128]{1,0:T(8,128)(2,1)} %w_ref.3) | copy-start | bytes 786436
  142.1 27.5 %all-to-all-start.6 = ((f32[8,32,128]{2,1,0:T(8,128)}), f32[8,32,128]{2,1,0:T(8,128)S(1)}, u32[]{:S(2)}, u32[]{:S(2)}) async-start(f32[8,32,128]{2,1,0:T(8,128)} %shard_map.101), calls=%async_computation.6 | async-start | bytes 262144 | tf_op jit(solution)/shard_map/all_to_all | solution.py:199
Sparse Core Ops, SparseCore 0:
  34.5 37.3 all-gather.3
  74.0 38.6 all-gather.5

commit v4 on v3

--- a/solution.py
+++ b/solution.py
@@ -198,6 +198,13 @@
     def swap(array, axis):
         return lax.all_to_all(array, axis, 0, 0, tiled=True)
 
+    def around(block, step, size):
+        got = [block]
+        for shift in (step, -step, 2 * step)[: size - 1]:
+            pairs = [(z, (z + shift) % nz) for z in range(nz)]
+            got.append(lax.ppermute(block, ("h", "l"), pairs))
+        return got
+
     def body(ctx_q, ctx_kv, anchor_kv, counts, offsets, query_in, w_query, w_out):
         rows = ctx_q.shape[0]
         heads = ctx_q.shape[1] // HD
@@ -223,21 +230,18 @@
             [ctx_kv.reshape(2 * rows, HD), jnp.broadcast_to(counts[0].astype(bf16), (16, HD))], axis=0
         )
         packed = swap(packed, "y")
-        window = [cache[None]]
-        for shift in (1, -1, 2)[: nl - 1]:
-            pairs = [(z, (z + shift) % nz) for z in range(nz)]
-            window.append(lax.ppermute(cache[None], ("h", "l"), pairs))
-        window, anchors = tie((jnp.concatenate(window, axis=0), anchor_kv[None]))
-        caches = lax.all_gather(window, "y", axis=0, tiled=True)
-        anchors = lax.all_gather(anchors, ("h", "l"), axis=0, tiled=True)
-        packed, anchors = tie((packed, anchors))
-        anchors = lax.all_gather(anchors, "y", axis=0, tiled=False)
+        packed, window = tie((packed, around(cache[None], 1, nl)))
+        caches = lax.all_gather(jnp.concatenate(window, axis=0), "y", axis=0, tiled=True)
 
         partial = kernel(
             functools.partial(project_kernel, depth, share), (nl, each, width), f32, packed
         )
         partial = swap(partial, "l")
+        partial, anchors = tie((partial, around(anchor_kv[None], nl, nh)))
+        anchors = jnp.concatenate(anchors, axis=0)
         partial = swap(spread(partial.sum(0), nh), "h")
+        partial, anchors = tie((partial, around(anchors, 1, nl)))
+        anchors = lax.all_gather(jnp.concatenate(anchors, axis=0), "y", axis=0, tiled=False)
         projected = partial.sum(0).astype(bf16)
 
         state = kernel(
@@ -254,19 +258,14 @@
         attend = lambda previous, index, steps: context_attention(
             ctx_q, ctx_kv, anchors, bounds, previous, index, steps
         )
-        attended, anchors = tie((attended, anchors))
         attended = swap(attended, "l")
-        ctx_attn = attend(None, 0, 1)
-        attended, ctx_attn = tie((attended, ctx_attn))
         attended = swap(spread(attended, ny), "y")
-        ctx_attn = attend(ctx_attn, 1, 1)
-        attended, ctx_attn = tie((attended, ctx_attn))
         product = kernel(
             functools.partial(output_kernel, share), (nt, qrows // nt, HD), f32, attended, w_out
         )
-        product, ctx_attn = tie((product, ctx_attn))
+        product, anchors = tie((product, anchors))
         product = swap(product, tp)
-        ctx_attn = attend(ctx_attn, 2, heads // 2 - 2)
+        ctx_attn = attend(None, 0, heads // 2)
         result = product.sum(0).astype(bf16)
         return (ctx_attn, result)
 

time: 178 us -> 182 us (1.022)
  blocking collectives: 72.9 us -> 29.4 us
  starting transfers between devices: 47 us -> 74.6 us
  waiting for transfers between devices: 11.4 us -> 32 us
  Pallas kernels: 21.9 us -> 19.7 us
    all_gather x1 -> x0, blocking collectives: 27.4 us -> none  [body(): anchors = lax.all_gather(anchors, ('h', 'l'), axis=0, tiled=True)]
    ppermute x3 -> x9, starting transfers between devices: 15.8 us -> 42.7 us  [around(): got.append(lax.ppermute(block, ('h', 'l'), pairs))]
    ppermute x3 -> x9, waiting for transfers between devices: 8.89 us -> 25.8 us  [around(): got.append(lax.ppermute(block, ('h', 'l'), pairs))]
    all_to_all x3 -> x2, blocking collectives: 45.5 us -> 29.4 us  [swap(): return lax.all_to_all(array, axis, 0, 0, tiled=True)]
    all_to_all x4 -> x5, waiting for transfers between devices: 2.42 us -> 6.22 us  [swap(): return lax.all_to_all(array, axis, 0, 0, tiled=True)]
    pallas_call x3 -> x1, Pallas kernels: 17.4 us -> 15.1 us  [context_attention(): pl.pallas_call(context_kernel, grid_spec=pltpu.PrefetchScalarGridSpec(num...]
    all_to_all x4 -> x5, starting transfers between devices: 31.2 us -> 31.9 us  [swap(): return lax.all_to_all(array, axis, 0, 0, tiled=True)]
    unnamed x18 -> x19, local copies, waits for them, and re-layouts: 5.01 us -> 5.01 us
  transfers between devices with their start and end apart: 9 -> 16, of which waited for: 3 -> 6; matrix products, arithmetic and copies ran while one was open for 0% -> 2% of each run, Pallas kernels for 12% -> 10%
where the time goes in v4:
time: 182 us; the launch traced here: 181 us
  starting transfers between devices  74.6 us (41%)
  waiting for transfers between devices  32 us (18%)
  blocking collectives  29.4 us (16%)
  Pallas kernels  19.7 us (11%)
  between operations  15.6 us (9%)
  local copies, waits for them, and re-layouts  7.53 us (4%)
  other arithmetic  2.47 us (1%)
    ppermute x9, starting transfers between devices, around(): got.append(lax.ppermute(block, ('h', 'l'), pairs))  42.7 us
    all_to_all x5, starting transfers between devices, swap(): return lax.all_to_all(array, axis, 0, 0, tiled=True)  31.9 us
    all_to_all x2, blocking collectives, swap(): return lax.all_to_all(array, axis, 0, 0, tiled=True)  29.4 us
    ppermute x9, waiting for transfers between devices, around(): got.append(lax.ppermute(block, ('h', 'l'), pairs))  25.8 us
    pallas_call x1, Pallas kernels, context_attention(): pl.pallas_call(context_kernel, grid_spec=pltpu.PrefetchScalarGridSpec(num...  15.1 us
    all_to_all x5, waiting for transfers between devices, swap(): return lax.all_to_all(array, axis, 0, 0, tiled=True)  6.22 us
    unnamed x19, local copies, waits for them, and re-layouts  5.01 us
    pallas_call x5, Pallas kernels, kernel(): pl.pallas_call(body, out_shape=jax.ShapeDtypeStruct(shape, dtype), compil...  4.52 us
  transfers between devices with their start and end apart: 16, of which 6 were waited for; matrix products, arithmetic and copies ran while one was open for 2% of the time, Pallas kernels for 10%

profile of v4, /device:TPU:1, one launch (start us, length us, event | category | flops | bytes accessed | tf_op | source)
XLA Modules:
  0.0 181.3 jit_solution(5738395171478754540)
XLA Ops:
  7.2 0.9 copy-done.2
  9.0 0.9 shard_map.95
  9.8 5.1 %all-to-all-start = ((bf16[4,512,128]{2,1,0:T(8,128)(2,1)}), bf16[4,512,128]{2,1,0:T(8,128)(2,1)S(1)}, u32[]{:S(2)}, u32[]{:S(2)}) async-start(bf16[4,512,128]{2,1,0:T(8,128)(2,1)} %shard_map.95), calls=%async_computation | async-start | bytes 1048576 | tf_op jit(solution)/shard_map/all_to_all | solution.py:199
  15.6 0.9 pad_bitcast_fusion
  16.5 3.5 %collective-permute-start = (bf16[1,528,128]{2,1,0:T(8,128)(2,1)S(1)}, bf16[1,528,128]{2,1,0:T(8,128)(2,1)S(1)}, u32[]{:S(2)}, u32[]{:S(2)}) collective-permute-start(bf16[1,528,128]{2,1,0:T(8,128)(2,1)S(1)} %pad_bitcast_fusion), channel_id=1, source_target_pairs={{0,8},{8,16},{16,24},{24,32},{32,40},{40,48},{48,56},{56,64},{64,7... | collective-permute-start | bytes 405512 | tf_op jit(solution)/shard_map/ppermute | solution.py:205
  20.1 9.5 %collective-permute-start.1 = (bf16[1,528,128]{2,1,0:T(8,128)(2,1)S(1)}, bf16[1,528,128]{2,1,0:T(8,128)(2,1)S(1)}, u32[]{:S(2)}, u32[]{:S(2)}) collective-permute-start(bf16[1,528,128]{2,1,0:T(8,128)(2,1)S(1)} %pad_bitcast_fusion), channel_id=1, source_target_pairs={{0,120},{8,0},{16,8},{24,16},{32,24},{40,32},{48,40},{56,48},{64,5... | collective-permute-start | bytes 405512 | tf_op jit(solution)/shard_map/ppermute | solution.py:205
  29.6 1.9 %collective-permute-start.2 = (bf16[1,528,128]{2,1,0:T(8,128)(2,1)S(1)}, bf16[1,528,128]{2,1,0:T(8,128)(2,1)S(1)}, u32[]{:S(2)}, u32[]{:S(2)}) collective-permute-start(bf16[1,528,128]{2,1,0:T(8,128)(2,1)S(1)} %pad_bitcast_fusion), channel_id=1, source_target_pairs={{0,16},{8,24},{16,32},{24,40},{32,48},{40,56},{48,64},{56,72},{64,... | collective-permute-start | bytes 405512 | tf_op jit(solution)/shard_map/ppermute | solution.py:205
  31.6 8.7 %collective-permute-done.2 = bf16[1,528,128]{2,1,0:T(8,128)(2,1)S(1)} collective-permute-done((bf16[1,528,128]{2,1,0:T(8,128)(2,1)S(1)}, bf16[1,528,128]{2,1,0:T(8,128)(2,1)S(1)}, u32[]{:S(2)}, u32[]{:S(2)}) %collective-permute-start.2) | collective-permute-done | bytes 135200 | tf_op jit(solution)/shard_map/ppermute | solution.py:205
  40.2 0.9 pad_maximum_fusion
  41.2 1.0 shard_map.96
  42.1 3.4 %all-to-all-start.1 = ((f32[4,64,256]{2,1,0:T(8,128)}), f32[4,64,256]{2,1,0:T(8,128)S(1)}, u32[]{:S(2)}, u32[]{:S(2)}) async-start(f32[4,64,256]{2,1,0:T(8,128)} %shard_map.96), calls=%async_computation.1 | async-start | bytes 524288 | tf_op jit(solution)/shard_map/all_to_all | solution.py:199
  45.6 3.0 %collective-permute-start.3 = (bf16[1,2,64,128]{3,2,1,0:T(8,128)(2,1)S(1)}, bf16[1,2,64,128]{3,2,1,0:T(8,128)(2,1)S(1)}, u32[]{:S(2)}, u32[]{:S(2)}) collective-permute-start(bf16[1,2,64,128]{3,2,1,0:T(8,128)(2,1)S(1)} %bitcast.8), channel_id=1, source_target_pairs={{0,32},{8,40},{16,48},{24,56},{32,64},{40,72},{48,80},{56,88},{64,... | collective-permute-start | bytes 98312 | tf_op jit(solution)/shard_map/ppermute | solution.py:205
  48.6 6.2 %collective-permute-start.4 = (bf16[1,2,64,128]{3,2,1,0:T(8,128)(2,1)S(1)}, bf16[1,2,64,128]{3,2,1,0:T(8,128)(2,1)S(1)}, u32[]{:S(2)}, u32[]{:S(2)}) collective-permute-start(bf16[1,2,64,128]{3,2,1,0:T(8,128)(2,1)S(1)} %bitcast.9), channel_id=1, source_target_pairs={{0,96},{8,104},{16,112},{24,120},{32,0},{40,8},{48,16},{56,24},{64... | collective-permute-start | bytes 98312 | tf_op jit(solution)/shard_map/ppermute | solution.py:205
  54.8 7.2 %collective-permute-start.5 = (bf16[1,2,64,128]{3,2,1,0:T(8,128)(2,1)S(1)}, bf16[1,2,64,128]{3,2,1,0:T(8,128)(2,1)S(1)}, u32[]{:S(2)}, u32[]{:S(2)}) collective-permute-start(bf16[1,2,64,128]{3,2,1,0:T(8,128)(2,1)S(1)} %bitcast.10), channel_id=1, source_target_pairs={{0,64},{8,72},{16,80},{24,88},{32,96},{40,104},{48,112},{56,120},{... | collective-permute-start | bytes 98312 | tf_op jit(solution)/shard_map/ppermute | solution.py:205
  62.0 6.2 %collective-permute-done.5 = bf16[1,2,64,128]{3,2,1,0:T(8,128)(2,1)S(1)} collective-permute-done((bf16[1,2,64,128]{3,2,1,0:T(8,128)(2,1)S(1)}, bf16[1,2,64,128]{3,2,1,0:T(8,128)(2,1)S(1)}, u32[]{:S(2)}, u32[]{:S(2)}) %collective-permute-start.5) | collective-permute-done | bytes 32800 | tf_op jit(solution)/shard_map/ppermute | solution.py:205
  68.9 6.5 %all-to-all-start.2 = ((f32[4,64,256]{2,1,0:T(8,128)}), f32[4,64,256]{2,1,0:T(8,128)S(1)}, u32[]{:S(2)}, u32[]{:S(2)}) async-start(f32[4,64,256]{2,1,0:T(8,128)} %broadcast_in_dim.10), calls=%async_computation.2 | async-start | bytes 524288 | tf_op jit(solution)/shard_map/all_to_all | solution.py:199
  75.5 3.4 %collective-permute-start.6 = (bf16[4,2,64,128]{3,2,1,0:T(8,128)(2,1)S(1)}, bf16[4,2,64,128]{3,2,1,0:T(8,128)(2,1)S(1)}, u32[]{:S(2)}, u32[]{:S(2)}) collective-permute-start(bf16[4,2,64,128]{3,2,1,0:T(8,128)(2,1)S(1)} %constant_dynamic-update-slice_fusion), channel_id=1, source_target_pairs={{0,8},{8,16},{16,24},{24,32},{32,40},{40,48},{48,56},{56,64},{64,7... | collective-permute-start | bytes 393224 | tf_op jit(solution)/shard_map/ppermute | solution.py:205
  78.9 6.1 %collective-permute-start.7 = (bf16[4,2,64,128]{3,2,1,0:T(8,128)(2,1)S(1)}, bf16[4,2,64,128]{3,2,1,0:T(8,128)(2,1)S(1)}, u32[]{:S(2)}, u32[]{:S(2)}) collective-permute-start(bf16[4,2,64,128]{3,2,1,0:T(8,128)(2,1)S(1)} %constant_dynamic-update-slice_fusion), channel_id=1, source_target_pairs={{0,120},{8,0},{16,8},{24,16},{32,24},{40,32},{48,40},{56,48},{64,5... | collective-permute-start | bytes 393224 | tf_op jit(solution)/shard_map/ppermute | solution.py:205
  85.0 1.9 %collective-permute-start.8 = (bf16[4,2,64,128]{3,2,1,0:T(8,128)(2,1)S(1)}, bf16[4,2,64,128]{3,2,1,0:T(8,128)(2,1)S(1)}, u32[]{:S(2)}, u32[]{:S(2)}) collective-permute-start(bf16[4,2,64,128]{3,2,1,0:T(8,128)(2,1)S(1)} %constant_dynamic-update-slice_fusion), channel_id=1, source_target_pairs={{0,16},{8,24},{16,32},{24,40},{32,48},{40,56},{48,64},{56,72},{64,... | collective-permute-start | bytes 393224 | tf_op jit(solution)/shard_map/ppermute | solution.py:205
  87.6 3.3 %collective-permute-done.7 = bf16[4,2,64,128]{3,2,1,0:T(8,128)(2,1)S(1)} collective-permute-done((bf16[4,2,64,128]{3,2,1,0:T(8,128)(2,1)S(1)}, bf16[4,2,64,128]{3,2,1,0:T(8,128)(2,1)S(1)}, u32[]{:S(2)}, u32[]{:S(2)}) %collective-permute-start.7) | collective-permute-done | bytes 131104 | tf_op jit(solution)/shard_map/ppermute | solution.py:205
  90.9 6.8 %collective-permute-done.8 = bf16[4,2,64,128]{3,2,1,0:T(8,128)(2,1)S(1)} collective-permute-done((bf16[4,2,64,128]{3,2,1,0:T(8,128)(2,1)S(1)}, bf16[4,2,64,128]{3,2,1,0:T(8,128)(2,1)S(1)}, u32[]{:S(2)}, u32[]{:S(2)}) %collective-permute-start.8) | collective-permute-done | bytes 131104 | tf_op jit(solution)/shard_map/ppermute | solution.py:205
  98.7 1.6 copy-done
  100.3 1.5 shard_map.97
  101.9 20.6 %all_to_all.35.in_ref = bf16[4,144,128]{2,1,0:T(8,128)(2,1)S(1)} all-to-all(bf16[4,144,128]{2,1,0:T(8,128)(2,1)S(1)} %shard_map.97), channel_id=1, replica_groups=mesh['y'=4,'h'=4,'l'=4,'x'=4,'c'=2] {'h'}, dimensions={0} | all-to-all | bytes 294912 | tf_op jit(solution)/shard_map/all_to_all | solution.py:199
  122.7 8.8 %all_to_all.36 = bf16[4,64,256]{2,1,0:T(8,128)(2,1)S(1)} all-to-all(bf16[4,64,256]{2,1,0:T(8,128)(2,1)S(1)} %shard_map.98), channel_id=1, replica_groups=mesh['y'=4,'h'=4,'l'=4,'x'=4,'c'=2] {'l'}, dimensions={0} | all-to-all | bytes 262144 | tf_op jit(solution)/shard_map/all_to_all | solution.py:199
  131.5 0.9 broadcast_in_dim.22
  132.4 7.5 %all-to-all-start.5 = ((bf16[4,4,64,256]{3,2,1,0:T(8,128)(2,1)}), bf16[4,4,64,256]{3,2,1,0:T(8,128)(2,1)S(1)}, u32[]{:S(2)}, u32[]{:S(2)}) async-start(bf16[4,4,64,256]{3,2,1,0:T(8,128)(2,1)} %broadcast_in_dim.22), calls=%async_computation.5 | async-start | bytes 1048576 | tf_op jit(solution)/shard_map/all_to_all | solution.py:199
  140.6 6.2 %all-to-all-done.5.att_ref = bf16[4,4,64,256]{3,2,1,0:T(8,128)(2,1)S(1)} async-done(((bf16[4,4,64,256]{3,2,1,0:T(8,128)(2,1)}), bf16[4,4,64,256]{3,2,1,0:T(8,128)(2,1)S(1)}, u32[]{:S(2)}, u32[]{:S(2)}) %all-to-all-start.5) | async-done | bytes 524320 | tf_op jit(solution)/shard_map/all_to_all | solution.py:199
  146.8 0.9 shard_map.99
  147.8 9.4 %all-to-all-start.6 = ((f32[8,32,128]{2,1,0:T(8,128)}), f32[8,32,128]{2,1,0:T(8,128)S(1)}, u32[]{:S(2)}, u32[]{:S(2)}) async-start(f32[8,32,128]{2,1,0:T(8,128)} %shard_map.99), calls=%async_computation.6 | async-start | bytes 262144 | tf_op jit(solution)/shard_map/all_to_all | solution.py:199
  157.1 1.6 copy-done.5
  158.7 15.1 %shard_map.100 = bf16[256,1024]{1,0:T(8,128)(2,1)} custom-call(s32[2]{0:T(128)S(1)} %pad_add_fusion.bounds, bf16[256,1024]{1,0:T(8,128)(2,1)S(1)} %copy-done.6, bf16[2,256,128]{2,1,0:T(8,128)(2,1)S(1)} %copy-done.3, bf16[4,16,2,64,128]{4,3,2,1,0:T(8,128)(2,1)S(1)} %bitcast.7), custom_call_target="tpu_custom_call" | custom-call | flops 9126805504 | bytes 2097152 | tf_op jit(solution)/shard_map/pallas_call | solution.py:69
  (39 shorter events, 4.2 us)
Async XLA Ops:
  7.2 1.0 copy-start.2
  8.1 0.8 copy-start.4
  9.8 35.7 %copy-start.7 = (bf16[2,64,128]{2,1,0:T(8,128)(2,1)S(1)}, bf16[2,64,128]{2,1,0:T(8,128)(2,1)}, u32[]{:S(2)}) copy-start(bf16[2,64,128]{2,1,0:T(8,128)(2,1)} %param.10) | copy-start | bytes 98308
  9.8 30.4 %all-to-all-start = ((bf16[4,512,128]{2,1,0:T(8,128)(2,1)}), bf16[4,512,128]{2,1,0:T(8,128)(2,1)S(1)}, u32[]{:S(2)}, u32[]{:S(2)}) async-start(bf16[4,512,128]{2,1,0:T(8,128)(2,1)} %shard_map.95), calls=%async_computation | async-start | bytes 1048576 | tf_op jit(solution)/shard_map/all_to_all | solution.py:199
  15.0 83.7 %all-gather.4.cloned.1.call-start = ((), (), s32[]{:S(2)}) async-start(), calls=%async_computation.7 | async-start | bytes 2703360 | tf_op jit(solution)/shard_map/all_gather | solution.py:234
  16.5 15.0 %collective-permute-start = (bf16[1,528,128]{2,1,0:T(8,128)(2,1)S(1)}, bf16[1,528,128]{2,1,0:T(8,128)(2,1)S(1)}, u32[]{:S(2)}, u32[]{:S(2)}) collective-permute-start(bf16[1,528,128]{2,1,0:T(8,128)(2,1)S(1)} %pad_bitcast_fusion), channel_id=1, source_target_pairs={{0,8},{8,16},{16,24},{24,32},{32,40},{40,48},{48,56},{56,64},{64,7... | collective-permute-start | bytes 405512 | tf_op jit(solution)/shard_map/ppermute | solution.py:205
  20.1 11.5 %collective-permute-start.1 = (bf16[1,528,128]{2,1,0:T(8,128)(2,1)S(1)}, bf16[1,528,128]{2,1,0:T(8,128)(2,1)S(1)}, u32[]{:S(2)}, u32[]{:S(2)}) collective-permute-start(bf16[1,528,128]{2,1,0:T(8,128)(2,1)S(1)} %pad_bitcast_fusion), channel_id=1, source_target_pairs={{0,120},{8,0},{16,8},{24,16},{32,24},{40,32},{48,40},{56,48},{64,5... | collective-permute-start | bytes 405512 | tf_op jit(solution)/shard_map/ppermute | solution.py:205
  29.6 10.6 %collective-permute-start.2 = (bf16[1,528,128]{2,1,0:T(8,128)(2,1)S(1)}, bf16[1,528,128]{2,1,0:T(8,128)(2,1)S(1)}, u32[]{:S(2)}, u32[]{:S(2)}) collective-permute-start(bf16[1,528,128]{2,1,0:T(8,128)(2,1)S(1)} %pad_bitcast_fusion), channel_id=1, source_target_pairs={{0,16},{8,24},{16,32},{24,40},{32,48},{40,56},{48,64},{56,72},{64,... | collective-permute-start | bytes 405512 | tf_op jit(solution)/shard_map/ppermute | solution.py:205
  42.1 26.1 %all-to-all-start.1 = ((f32[4,64,256]{2,1,0:T(8,128)}), f32[4,64,256]{2,1,0:T(8,128)S(1)}, u32[]{:S(2)}, u32[]{:S(2)}) async-start(f32[4,64,256]{2,1,0:T(8,128)} %shard_map.96), calls=%async_computation.1 | async-start | bytes 524288 | tf_op jit(solution)/shard_map/all_to_all | solution.py:199
  45.6 16.4 %collective-permute-start.3 = (bf16[1,2,64,128]{3,2,1,0:T(8,128)(2,1)S(1)}, bf16[1,2,64,128]{3,2,1,0:T(8,128)(2,1)S(1)}, u32[]{:S(2)}, u32[]{:S(2)}) collective-permute-start(bf16[1,2,64,128]{3,2,1,0:T(8,128)(2,1)S(1)} %bitcast.8), channel_id=1, source_target_pairs={{0,32},{8,40},{16,48},{24,56},{32,64},{40,72},{48,80},{56,88},{64,... | collective-permute-start | bytes 98312 | tf_op jit(solution)/shard_map/ppermute | solution.py:205
  48.6 13.4 %collective-permute-start.4 = (bf16[1,2,64,128]{3,2,1,0:T(8,128)(2,1)S(1)}, bf16[1,2,64,128]{3,2,1,0:T(8,128)(2,1)S(1)}, u32[]{:S(2)}, u32[]{:S(2)}) collective-permute-start(bf16[1,2,64,128]{3,2,1,0:T(8,128)(2,1)S(1)} %bitcast.9), channel_id=1, source_target_pairs={{0,96},{8,104},{16,112},{24,120},{32,0},{40,8},{48,16},{56,24},{64... | collective-permute-start | bytes 98312 | tf_op jit(solution)/shard_map/ppermute | solution.py:205
  54.8 13.4 %collective-permute-start.5 = (bf16[1,2,64,128]{3,2,1,0:T(8,128)(2,1)S(1)}, bf16[1,2,64,128]{3,2,1,0:T(8,128)(2,1)S(1)}, u32[]{:S(2)}, u32[]{:S(2)}) collective-permute-start(bf16[1,2,64,128]{3,2,1,0:T(8,128)(2,1)S(1)} %bitcast.10), channel_id=1, source_target_pairs={{0,64},{8,72},{16,80},{24,88},{32,96},{40,104},{48,112},{56,120},{... | collective-permute-start | bytes 98312 | tf_op jit(solution)/shard_map/ppermute | solution.py:205
  68.9 28.8 %all-to-all-start.2 = ((f32[4,64,256]{2,1,0:T(8,128)}), f32[4,64,256]{2,1,0:T(8,128)S(1)}, u32[]{:S(2)}, u32[]{:S(2)}) async-start(f32[4,64,256]{2,1,0:T(8,128)} %broadcast_in_dim.10), calls=%async_computation.2 | async-start | bytes 524288 | tf_op jit(solution)/shard_map/all_to_all | solution.py:199
  75.4 72.3 %all-gather.6.cloned.1.call-start = ((), (), s32[]{:S(2)}) async-start(), calls=%async_computation.8 | async-start | bytes 2621440 | tf_op jit(solution)/shard_map/all_gather | solution.py:244
  75.5 12.1 %collective-permute-start.6 = (bf16[4,2,64,128]{3,2,1,0:T(8,128)(2,1)S(1)}, bf16[4,2,64,128]{3,2,1,0:T(8,128)(2,1)S(1)}, u32[]{:S(2)}, u32[]{:S(2)}) collective-permute-start(bf16[4,2,64,128]{3,2,1,0:T(8,128)(2,1)S(1)} %constant_dynamic-update-slice_fusion), channel_id=1, source_target_pairs={{0,8},{8,16},{16,24},{24,32},{32,40},{40,48},{48,56},{56,64},{64,7... | collective-permute-start | bytes 393224 | tf_op jit(solution)/shard_map/ppermute | solution.py:205
  78.9 12.0 %collective-permute-start.7 = (bf16[4,2,64,128]{3,2,1,0:T(8,128)(2,1)S(1)}, bf16[4,2,64,128]{3,2,1,0:T(8,128)(2,1)S(1)}, u32[]{:S(2)}, u32[]{:S(2)}) collective-permute-start(bf16[4,2,64,128]{3,2,1,0:T(8,128)(2,1)S(1)} %constant_dynamic-update-slice_fusion), channel_id=1, source_target_pairs={{0,120},{8,0},{16,8},{24,16},{32,24},{40,32},{48,40},{56,48},{64,5... | collective-permute-start | bytes 393224 | tf_op jit(solution)/shard_map/ppermute | solution.py:205
  85.0 12.8 %collective-permute-start.8 = (bf16[4,2,64,128]{3,2,1,0:T(8,128)(2,1)S(1)}, bf16[4,2,64,128]{3,2,1,0:T(8,128)(2,1)S(1)}, u32[]{:S(2)}, u32[]{:S(2)}) collective-permute-start(bf16[4,2,64,128]{3,2,1,0:T(8,128)(2,1)S(1)} %constant_dynamic-update-slice_fusion), channel_id=1, source_target_pairs={{0,16},{8,24},{16,32},{24,40},{32,48},{40,56},{48,64},{56,72},{64,... | collective-permute-start | bytes 393224 | tf_op jit(solution)/shard_map/ppermute | solution.py:205
  98.7 1.6 copy-start
  100.3 46.5 %copy-start.1 = (bf16[1024,128]{1,0:T(8,128)(2,1)S(1)}, bf16[1024,128]{1,0:T(8,128)(2,1)}, u32[]{:S(2)}) copy-start(bf16[1024,128]{1,0:T(8,128)(2,1)} %w_ref.3) | copy-start | bytes 786436
  101.9 55.2 %copy-start.3 = (bf16[2,256,128]{2,1,0:T(8,128)(2,1)S(1)}, bf16[2,256,128]{2,1,0:T(8,128)(2,1)}, u32[]{:S(2)}) copy-start(bf16[2,256,128]{2,1,0:T(8,128)(2,1)} %own_ref.1) | copy-start | bytes 393220
  101.9 55.2 %copy-start.6 = (bf16[256,1024]{1,0:T(8,128)(2,1)S(1)}, bf16[256,1024]{1,0:T(8,128)(2,1)}, u32[]{:S(2)}) copy-start(bf16[256,1024]{1,0:T(8,128)(2,1)} %q_ref.3) | copy-start | bytes 1572868
  132.4 14.4 %all-to-all-start.5 = ((bf16[4,4,64,256]{3,2,1,0:T(8,128)(2,1)}), bf16[4,4,64,256]{3,2,1,0:T(8,128)(2,1)S(1)}, u32[]{:S(2)}, u32[]{:S(2)}) async-start(bf16[4,4,64,256]{3,2,1,0:T(8,128)(2,1)} %broadcast_in_dim.22), calls=%async_computation.5 | async-start | bytes 1048576 | tf_op jit(solution)/shard_map/all_to_all | solution.py:199
  147.8 26.1 %all-to-all-start.6 = ((f32[8,32,128]{2,1,0:T(8,128)}), f32[8,32,128]{2,1,0:T(8,128)S(1)}, u32[]{:S(2)}, u32[]{:S(2)}) async-start(f32[8,32,128]{2,1,0:T(8,128)} %shard_map.99), calls=%async_computation.6 | async-start | bytes 262144 | tf_op jit(solution)/shard_map/all_to_all | solution.py:199
  157.1 1.6 copy-start.5
Sparse Core Ops, SparseCore 0:
  41.3 37.6 all-gather.3
  98.8 39.6 all-gather.5

commit v5 on v4

--- a/solution.py
+++ b/solution.py
@@ -236,12 +236,12 @@
         partial = kernel(
             functools.partial(project_kernel, depth, share), (nl, each, width), f32, packed
         )
+        partial, anchors = tie((partial, anchor_kv[None]))
         partial = swap(partial, "l")
-        partial, anchors = tie((partial, around(anchor_kv[None], nl, nh)))
-        anchors = jnp.concatenate(anchors, axis=0)
+        anchors = lax.all_gather(anchors, ("h", "l"), axis=0, tiled=True)
+        partial, anchors = tie((partial, anchors))
+        anchors = lax.all_gather(anchors, "y", axis=0, tiled=False)
         partial = swap(spread(partial.sum(0), nh), "h")
-        partial, anchors = tie((partial, around(anchors, 1, nl)))
-        anchors = lax.all_gather(jnp.concatenate(anchors, axis=0), "y", axis=0, tiled=False)
         projected = partial.sum(0).astype(bf16)
 
         state = kernel(
@@ -258,14 +258,19 @@
         attend = lambda previous, index, steps: context_attention(
             ctx_q, ctx_kv, anchors, bounds, previous, index, steps
         )
+        attended, anchors = tie((attended, anchors))
         attended = swap(attended, "l")
+        ctx_attn = attend(None, 0, 1)
+        attended, ctx_attn = tie((attended, ctx_attn))
         attended = swap(spread(attended, ny), "y")
+        ctx_attn = attend(ctx_attn, 1, 1)
+        attended, ctx_attn = tie((attended, ctx_attn))
         product = kernel(
             functools.partial(output_kernel, share), (nt, qrows // nt, HD), f32, attended, w_out
         )
-        product, anchors = tie((product, anchors))
+        product, ctx_attn = tie((product, ctx_attn))
         product = swap(product, tp)
-        ctx_attn = attend(None, 0, heads // 2)
+        ctx_attn = attend(ctx_attn, 2, heads // 2 - 2)
         result = product.sum(0).astype(bf16)
         return (ctx_attn, result)
 

time: 182 us -> 172 us (0.945)
  blocking collectives: 29.4 us -> 65.6 us
  starting transfers between devices: 74.6 us -> 43.6 us
  waiting for transfers between devices: 32 us -> 15.3 us
  Pallas kernels: 19.7 us -> 22.6 us
    all_gather x0 -> x1, blocking collectives: none -> 29.8 us  [body(): anchors = lax.all_gather(anchors, ('h', 'l'), axis=0, tiled=True)]
    ppermute x9 -> x3, starting transfers between devices: 42.7 us -> 15 us  [around(): got.append(lax.ppermute(block, ('h', 'l'), pairs))]
    ppermute x9 -> x3, waiting for transfers between devices: 25.8 us -> 8.7 us  [around(): got.append(lax.ppermute(block, ('h', 'l'), pairs))]
    all_to_all x2, blocking collectives: 29.4 us -> 35.8 us  [swap(): return lax.all_to_all(array, axis, 0, 0, tiled=True)]
    all_gather x1, waiting for transfers between devices: 0.01 us -> 4.32 us  [body(): anchors = lax.all_gather(anchors, 'y', axis=0, tiled=False)]
    all_to_all x5, waiting for transfers between devices: 6.22 us -> 2.23 us  [swap(): return lax.all_to_all(array, axis, 0, 0, tiled=True)]
    all_to_all x5, starting transfers between devices: 31.9 us -> 28.6 us  [swap(): return lax.all_to_all(array, axis, 0, 0, tiled=True)]
    pallas_call x1 -> x3, Pallas kernels: 15.1 us -> 17.4 us  [context_attention(): pl.pallas_call(context_kernel, grid_spec=pltpu.PrefetchScalarGridSpec(num...]
  transfers between devices with their start and end apart: 16 -> 10, of which waited for: 6 -> 3; matrix products, arithmetic and copies ran while one was open for 2% -> 1% of each run, Pallas kernels for 10% -> 12%
where the time goes in v5:
time: 172 us; the launch traced here: 171 us
  blocking collectives  65.6 us (38%)
  starting transfers between devices  43.6 us (25%)
  Pallas kernels  22.6 us (13%)
  between operations  15.5 us (9%)
  waiting for transfers between devices  15.3 us (9%)
  local copies, waits for them, and re-layouts  6.79 us (4%)
    all_to_all x2, blocking collectives, swap(): return lax.all_to_all(array, axis, 0, 0, tiled=True)  35.8 us
    all_gather x1, blocking collectives, body(): anchors = lax.all_gather(anchors, ('h', 'l'), axis=0, tiled=True)  29.8 us
    all_to_all x5, starting transfers between devices, swap(): return lax.all_to_all(array, axis, 0, 0, tiled=True)  28.6 us
    pallas_call x3, Pallas kernels, context_attention(): pl.pallas_call(context_kernel, grid_spec=pltpu.PrefetchScalarGridSpec(num...  17.4 us
    ppermute x3, starting transfers between devices, around(): got.append(lax.ppermute(block, ('h', 'l'), pairs))  15 us
    ppermute x3, waiting for transfers between devices, around(): got.append(lax.ppermute(block, ('h', 'l'), pairs))  8.7 us
    pallas_call x5, Pallas kernels, kernel(): pl.pallas_call(body, out_shape=jax.ShapeDtypeStruct(shape, dtype), compil...  5.19 us
    unnamed x18, local copies, waits for them, and re-layouts  5 us
  transfers between devices with their start and end apart: 10, of which 3 were waited for; matrix products, arithmetic and copies ran while one was open for 1% of the time, Pallas kernels for 12%

profile of v5, /device:TPU:1, one launch (start us, length us, event | category | flops | bytes accessed | tf_op | source)
XLA Modules:
  0.0 171.0 jit_solution(1091831597898492134)
XLA Ops:
  7.2 0.9 copy-done.2
  8.1 0.8 copy-done.4
  9.0 0.9 shard_map.95
  9.8 5.1 %all-to-all-start = ((bf16[4,512,128]{2,1,0:T(8,128)(2,1)}), bf16[4,512,128]{2,1,0:T(8,128)(2,1)S(1)}, u32[]{:S(2)}, u32[]{:S(2)}) async-start(bf16[4,512,128]{2,1,0:T(8,128)(2,1)} %shard_map.95), calls=%async_computation | async-start | bytes 1048576 | tf_op jit(solution)/shard_map/all_to_all | solution.py:199
  15.6 0.9 pad_bitcast_fusion
  16.5 3.5 %collective-permute-start = (bf16[1,528,128]{2,1,0:T(8,128)(2,1)S(1)}, bf16[1,528,128]{2,1,0:T(8,128)(2,1)S(1)}, u32[]{:S(2)}, u32[]{:S(2)}) collective-permute-start(bf16[1,528,128]{2,1,0:T(8,128)(2,1)S(1)} %pad_bitcast_fusion), channel_id=1, source_target_pairs={{0,8},{8,16},{16,24},{24,32},{32,40},{40,48},{48,56},{56,64},{64,7... | collective-permute-start | bytes 405512 | tf_op jit(solution)/shard_map/ppermute | solution.py:205
  20.1 9.5 %collective-permute-start.1 = (bf16[1,528,128]{2,1,0:T(8,128)(2,1)S(1)}, bf16[1,528,128]{2,1,0:T(8,128)(2,1)S(1)}, u32[]{:S(2)}, u32[]{:S(2)}) collective-permute-start(bf16[1,528,128]{2,1,0:T(8,128)(2,1)S(1)} %pad_bitcast_fusion), channel_id=1, source_target_pairs={{0,120},{8,0},{16,8},{24,16},{32,24},{40,32},{48,40},{56,48},{64,5... | collective-permute-start | bytes 405512 | tf_op jit(solution)/shard_map/ppermute | solution.py:205
  29.6 1.9 %collective-permute-start.2 = (bf16[1,528,128]{2,1,0:T(8,128)(2,1)S(1)}, bf16[1,528,128]{2,1,0:T(8,128)(2,1)S(1)}, u32[]{:S(2)}, u32[]{:S(2)}) collective-permute-start(bf16[1,528,128]{2,1,0:T(8,128)(2,1)S(1)} %pad_bitcast_fusion), channel_id=1, source_target_pairs={{0,16},{8,24},{16,32},{24,40},{32,48},{40,56},{48,64},{56,72},{64,... | collective-permute-start | bytes 405512 | tf_op jit(solution)/shard_map/ppermute | solution.py:205
  31.6 8.7 %collective-permute-done.2 = bf16[1,528,128]{2,1,0:T(8,128)(2,1)S(1)} collective-permute-done((bf16[1,528,128]{2,1,0:T(8,128)(2,1)S(1)}, bf16[1,528,128]{2,1,0:T(8,128)(2,1)S(1)}, u32[]{:S(2)}, u32[]{:S(2)}) %collective-permute-start.2) | collective-permute-done | bytes 135200 | tf_op jit(solution)/shard_map/ppermute | solution.py:205
  40.2 0.9 pad_maximum_fusion
  41.1 1.0 shard_map.96
  42.1 3.4 %all-to-all-start.1 = ((f32[4,64,256]{2,1,0:T(8,128)}), f32[4,64,256]{2,1,0:T(8,128)S(1)}, u32[]{:S(2)}, u32[]{:S(2)}) async-start(f32[4,64,256]{2,1,0:T(8,128)} %shard_map.96), calls=%async_computation.1 | async-start | bytes 524288 | tf_op jit(solution)/shard_map/all_to_all | solution.py:199
  45.6 0.0 all-gather.6.cloned.1.call-start
  45.6 29.8 %all_gather.12 = bf16[16,2,64,128]{3,2,1,0:T(8,128)(2,1)} all-gather(bf16[1,2,64,128]{3,2,1,0:T(8,128)(2,1)S(1)} %bitcast.10), channel_id=1, replica_groups=mesh['y'=4,'h'=4,'l'=4,'x'=4,'c'=2] {'h','l'}, dimensions={0}, use_global_device_ids=true | all-gather | bytes 557056 | tf_op jit(solution)/shard_map/all_gather | solution.py:241
  75.5 19.0 %all_to_all.35 = f32[4,64,256]{2,1,0:T(8,128)S(1)} all-to-all(f32[4,64,256]{2,1,0:T(8,128)S(1)} %broadcast_in_dim.10), channel_id=1, replica_groups=mesh['y'=4,'h'=4,'l'=4,'x'=4,'c'=2] {'h'}, dimensions={0} | all-to-all | bytes 524288 | tf_op jit(solution)/shard_map/all_to_all | solution.py:199
  94.5 1.6 copy-done
  96.1 1.6 shard_map.97
  97.7 16.9 %all_to_all.36.in_ref = bf16[4,144,128]{2,1,0:T(8,128)(2,1)S(1)} all-to-all(bf16[4,144,128]{2,1,0:T(8,128)(2,1)S(1)} %shard_map.97), channel_id=1, replica_groups=mesh['y'=4,'h'=4,'l'=4,'x'=4,'c'=2] {'h'}, dimensions={0} | all-to-all | bytes 294912 | tf_op jit(solution)/shard_map/all_to_all | solution.py:199
  114.5 0.8 shard_map.98
  115.4 4.3 %all-gather.6.cloned.1.call-done = bf16[64,2,64,128]{3,2,1,0:T(8,128)(2,1)} async-done(((bf16[16,2,64,128]{3,2,1,0:T(8,128)(2,1)}), bf16[64,2,64,128]{3,2,1,0:T(8,128)(2,1)}) %all-gather.6.cloned.1.call-update) | async-done | bytes 2097168 | tf_op jit(solution)/shard_map/all_gather | solution.py:243
  119.7 4.5 %all-to-all-start.4 = ((bf16[4,64,256]{2,1,0:T(8,128)(2,1)}), bf16[4,64,256]{2,1,0:T(8,128)(2,1)S(1)}, u32[]{:S(2)}, u32[]{:S(2)}) async-start(bf16[4,64,256]{2,1,0:T(8,128)(2,1)} %shard_map.98), calls=%async_computation.4 | async-start | bytes 262144 | tf_op jit(solution)/shard_map/all_to_all | solution.py:199
  124.9 0.1 pad_add_fusion.bounds
  125.0 1.6 copy-done.5
  126.6 4.6 %shard_map.99.rest_0_ = bf16[256,1024]{1,0:T(8,128)(2,1)} custom-call(s32[2]{0:T(128)S(1)} %pad_add_fusion.bounds, bf16[256,1024]{1,0:T(8,128)(2,1)S(1)} %copy-done.7, bf16[2,256,128]{2,1,0:T(8,128)(2,1)S(1)} %copy-done.3, bf16[4,16,2,64,128]{4,3,2,1,0:T(8,128)(2,1)S(1)} %bitcast.7), custom_call_target="tpu_custom_call" | custom-call | flops 2281701376 | bytes 2097152 | tf_op jit(solution)/shard_map/pallas_call | solution.py:69
  131.2 0.9 broadcast_in_dim.22
  132.0 3.5 %all-to-all-start.5 = ((bf16[4,4,64,256]{3,2,1,0:T(8,128)(2,1)}), bf16[4,4,64,256]{3,2,1,0:T(8,128)(2,1)S(1)}, u32[]{:S(2)}, u32[]{:S(2)}) async-start(bf16[4,4,64,256]{3,2,1,0:T(8,128)(2,1)} %broadcast_in_dim.22), calls=%async_computation.5 | async-start | bytes 1048576 | tf_op jit(solution)/shard_map/all_to_all | solution.py:199
  135.5 4.7 %shard_map.100.rest_0_ = bf16[256,1024]{1,0:T(8,128)(2,1)} custom-call(s32[2]{0:T(128)S(1)} %pad_add_fusion.bounds, bf16[256,1024]{1,0:T(8,128)(2,1)S(1)} %copy-done.7, bf16[2,256,128]{2,1,0:T(8,128)(2,1)S(1)} %copy-done.3, bf16[4,16,2,64,128]{4,3,2,1,0:T(8,128)(2,1)S(1)} %bitcast.8, bf16[256,1024]{1,0:T(8,128)(2,1)} %shard_map.99.rest_0_), custom_call_target="tpu_custom_call", output_to_operand_aliasing={{}: (4, {})} | custom-call | flops 2281701376 | bytes 2097152 | tf_op jit(solution)/shard_map/pallas_call | solution.py:69
  140.2 2.2 %all-to-all-done.5.att_ref = bf16[4,4,64,256]{3,2,1,0:T(8,128)(2,1)S(1)} async-done(((bf16[4,4,64,256]{3,2,1,0:T(8,128)(2,1)}), bf16[4,4,64,256]{3,2,1,0:T(8,128)(2,1)S(1)}, u32[]{:S(2)}, u32[]{:S(2)}) %all-to-all-start.5) | async-done | bytes 524320 | tf_op jit(solution)/shard_map/all_to_all | solution.py:199
  142.4 0.9 shard_map.101
  143.3 12.0 %all-to-all-start.6 = ((f32[8,32,128]{2,1,0:T(8,128)}), f32[8,32,128]{2,1,0:T(8,128)S(1)}, u32[]{:S(2)}, u32[]{:S(2)}) async-start(f32[8,32,128]{2,1,0:T(8,128)} %shard_map.101), calls=%async_computation.6 | async-start | bytes 262144 | tf_op jit(solution)/shard_map/all_to_all | solution.py:199
  155.3 8.2 %shard_map.102 = bf16[256,1024]{1,0:T(8,128)(2,1)} custom-call(s32[2]{0:T(128)S(1)} %pad_add_fusion.bounds, bf16[256,1024]{1,0:T(8,128)(2,1)S(1)} %copy-done.7, bf16[2,256,128]{2,1,0:T(8,128)(2,1)S(1)} %copy-done.3, bf16[4,16,2,64,128]{4,3,2,1,0:T(8,128)(2,1)S(1)} %bitcast.9, bf16[256,1024]{1,0:T(8,128)(2,1)} %shard_map.100.rest_0_), custom_call_target="tpu_custom_call", output_to_operand_aliasing={{}: (4, {})} | custom-call | flops 4563402752 | bytes 2097152 | tf_op jit(solution)/shard_map/pallas_call | solution.py:69
  163.5 0.6 reduce_sum.29
  (27 shorter events, 0.2 us)
Async XLA Ops:
  7.2 1.0 copy-start.2
  8.1 0.8 copy-start.4
  9.8 35.8 %copy-start.8 = (bf16[2,64,128]{2,1,0:T(8,128)(2,1)S(1)}, bf16[2,64,128]{2,1,0:T(8,128)(2,1)}, u32[]{:S(2)}) copy-start(bf16[2,64,128]{2,1,0:T(8,128)(2,1)} %param.10) | copy-start | bytes 98308
  9.8 30.4 %all-to-all-start = ((bf16[4,512,128]{2,1,0:T(8,128)(2,1)}), bf16[4,512,128]{2,1,0:T(8,128)(2,1)S(1)}, u32[]{:S(2)}, u32[]{:S(2)}) async-start(bf16[4,512,128]{2,1,0:T(8,128)(2,1)} %shard_map.95), calls=%async_computation | async-start | bytes 1048576 | tf_op jit(solution)/shard_map/all_to_all | solution.py:199
  15.0 79.5 %all-gather.4.cloned.1.call-start = ((), (), s32[]{:S(2)}) async-start(), calls=%async_computation.7 | async-start | bytes 2703360 | tf_op jit(solution)/shard_map/all_gather | solution.py:234
  16.5 15.0 %collective-permute-start = (bf16[1,528,128]{2,1,0:T(8,128)(2,1)S(1)}, bf16[1,528,128]{2,1,0:T(8,128)(2,1)S(1)}, u32[]{:S(2)}, u32[]{:S(2)}) collective-permute-start(bf16[1,528,128]{2,1,0:T(8,128)(2,1)S(1)} %pad_bitcast_fusion), channel_id=1, source_target_pairs={{0,8},{8,16},{16,24},{24,32},{32,40},{40,48},{48,56},{56,64},{64,7... | collective-permute-start | bytes 405512 | tf_op jit(solution)/shard_map/ppermute | solution.py:205
  20.1 11.5 %collective-permute-start.1 = (bf16[1,528,128]{2,1,0:T(8,128)(2,1)S(1)}, bf16[1,528,128]{2,1,0:T(8,128)(2,1)S(1)}, u32[]{:S(2)}, u32[]{:S(2)}) collective-permute-start(bf16[1,528,128]{2,1,0:T(8,128)(2,1)S(1)} %pad_bitcast_fusion), channel_id=1, source_target_pairs={{0,120},{8,0},{16,8},{24,16},{32,24},{40,32},{48,40},{56,48},{64,5... | collective-permute-start | bytes 405512 | tf_op jit(solution)/shard_map/ppermute | solution.py:205
  29.6 10.6 %collective-permute-start.2 = (bf16[1,528,128]{2,1,0:T(8,128)(2,1)S(1)}, bf16[1,528,128]{2,1,0:T(8,128)(2,1)S(1)}, u32[]{:S(2)}, u32[]{:S(2)}) collective-permute-start(bf16[1,528,128]{2,1,0:T(8,128)(2,1)S(1)} %pad_bitcast_fusion), channel_id=1, source_target_pairs={{0,16},{8,24},{16,32},{24,40},{32,48},{40,56},{48,64},{56,72},{64,... | collective-permute-start | bytes 405512 | tf_op jit(solution)/shard_map/ppermute | solution.py:205
  42.1 33.2 %all-to-all-start.1 = ((f32[4,64,256]{2,1,0:T(8,128)}), f32[4,64,256]{2,1,0:T(8,128)S(1)}, u32[]{:S(2)}, u32[]{:S(2)}) async-start(f32[4,64,256]{2,1,0:T(8,128)} %shard_map.96), calls=%async_computation.1 | async-start | bytes 524288 | tf_op jit(solution)/shard_map/all_to_all | solution.py:199
  45.6 74.1 %all-gather.6.cloned.1.call-start = ((), (), s32[]{:S(2)}) async-start(), calls=%async_computation.8 | async-start | bytes 2621440 | tf_op jit(solution)/shard_map/all_gather | solution.py:243
  75.4 49.5 %copy-start.3 = (bf16[2,256,128]{2,1,0:T(8,128)(2,1)S(1)}, bf16[2,256,128]{2,1,0:T(8,128)(2,1)}, u32[]{:S(2)}) copy-start(bf16[2,256,128]{2,1,0:T(8,128)(2,1)} %own_ref.5) | copy-start | bytes 393220
  75.4 49.5 %copy-start.7 = (bf16[256,1024]{1,0:T(8,128)(2,1)S(1)}, bf16[256,1024]{1,0:T(8,128)(2,1)}, u32[]{:S(2)}) copy-start(bf16[256,1024]{1,0:T(8,128)(2,1)} %q_ref.7) | copy-start | bytes 1572868
  94.5 1.6 copy-start
  119.7 11.5 %all-to-all-start.4 = ((bf16[4,64,256]{2,1,0:T(8,128)(2,1)}), bf16[4,64,256]{2,1,0:T(8,128)(2,1)S(1)}, u32[]{:S(2)}, u32[]{:S(2)}) async-start(bf16[4,64,256]{2,1,0:T(8,128)(2,1)} %shard_map.98), calls=%async_computation.4 | async-start | bytes 262144 | tf_op jit(solution)/shard_map/all_to_all | solution.py:199
  125.0 1.6 copy-start.5
  126.5 8.9 %copy-start.6 = (bf16[64,2,64,128]{3,2,1,0:T(8,128)(2,1)S(1)}, bf16[64,2,64,128]{3,2,1,0:T(8,128)(2,1)}, u32[]{:S(2)}) copy-start(bf16[64,2,64,128]{3,2,1,0:T(8,128)(2,1)} %all-gather.6.cloned.1.call-done) | copy-start | bytes 6291460
  132.0 10.4 %all-to-all-start.5 = ((bf16[4,4,64,256]{3,2,1,0:T(8,128)(2,1)}), bf16[4,4,64,256]{3,2,1,0:T(8,128)(2,1)S(1)}, u32[]{:S(2)}, u32[]{:S(2)}) async-start(bf16[4,4,64,256]{3,2,1,0:T(8,128)(2,1)} %broadcast_in_dim.22), calls=%async_computation.5 | async-start | bytes 1048576 | tf_op jit(solution)/shard_map/all_to_all | solution.py:199
  135.5 6.9 %copy-start.1 = (bf16[1024,128]{1,0:T(8,128)(2,1)S(1)}, bf16[1024,128]{1,0:T(8,128)(2,1)}, u32[]{:S(2)}) copy-start(bf16[1024,128]{1,0:T(8,128)(2,1)} %w_ref.3) | copy-start | bytes 786436
  143.3 20.2 %all-to-all-start.6 = ((f32[8,32,128]{2,1,0:T(8,128)}), f32[8,32,128]{2,1,0:T(8,128)S(1)}, u32[]{:S(2)}, u32[]{:S(2)}) async-start(f32[8,32,128]{2,1,0:T(8,128)} %shard_map.101), calls=%async_computation.6 | async-start | bytes 262144 | tf_op jit(solution)/shard_map/all_to_all | solution.py:199
Sparse Core Ops, SparseCore 0:
  41.3 37.6 all-gather.3
  81.0 38.6 all-gather.5

commit v6 on v5

--- a/solution.py
+++ b/solution.py
@@ -238,10 +238,12 @@
         )
         partial, anchors = tie((partial, anchor_kv[None]))
         partial = swap(partial, "l")
-        anchors = lax.all_gather(anchors, ("h", "l"), axis=0, tiled=True)
+        anchors = lax.all_gather(anchors, "h", axis=0, tiled=True)
+        partial, anchors = tie((partial, anchors))
+        partial = swap(spread(partial.sum(0), nh), "h")
+        anchors = lax.all_gather(anchors, "l", axis=0, tiled=True)
         partial, anchors = tie((partial, anchors))
         anchors = lax.all_gather(anchors, "y", axis=0, tiled=False)
-        partial = swap(spread(partial.sum(0), nh), "h")
         projected = partial.sum(0).astype(bf16)
 
         state = kernel(
@@ -258,19 +260,17 @@
         attend = lambda previous, index, steps: context_attention(
             ctx_q, ctx_kv, anchors, bounds, previous, index, steps
         )
+        attended = swap(attended, "l")
         attended, anchors = tie((attended, anchors))
-        attended = swap(attended, "l")
+        attended = swap(spread(attended, ny), "y")
         ctx_attn = attend(None, 0, 1)
-        attended, ctx_attn = tie((attended, ctx_attn))
-        attended = swap(spread(attended, ny), "y")
-        ctx_attn = attend(ctx_attn, 1, 1)
         attended, ctx_attn = tie((attended, ctx_attn))
         product = kernel(
             functools.partial(output_kernel, share), (nt, qrows // nt, HD), f32, attended, w_out
         )
         product, ctx_attn = tie((product, ctx_attn))
         product = swap(product, tp)
-        ctx_attn = attend(ctx_attn, 2, heads // 2 - 2)
+        ctx_attn = attend(ctx_attn, 1, heads // 2 - 1)
         result = product.sum(0).astype(bf16)
         return (ctx_attn, result)
 

time: 172 us -> 175 us (1.017)
  waiting for transfers between devices: 15.3 us -> 22.6 us
  starting transfers between devices: 43.6 us -> 39.2 us
  blocking collectives: 65.6 us -> 67.6 us
  Pallas kernels: 22.6 us -> 20.7 us
    all_gather x1, waiting for transfers between devices: 4.32 us -> 12 us  [body(): anchors = lax.all_gather(anchors, 'y', axis=0, tiled=False)]
    all_gather x1 -> x2, blocking collectives: 29.8 us -> 36.2 us  [the longest x1 21.2 us: body(): anchors = lax.all_gather(anchors, 'l', axis=0, tiled=True)]
    all_to_all x2, blocking collectives: 35.8 us -> 31.4 us  [swap(): return lax.all_to_all(array, axis, 0, 0, tiled=True)]
    all_to_all x5, starting transfers between devices: 28.6 us -> 24.2 us  [swap(): return lax.all_to_all(array, axis, 0, 0, tiled=True)]
    pallas_call x3 -> x2, Pallas kernels: 17.4 us -> 16.2 us  [context_attention(): pl.pallas_call(context_kernel, grid_spec=pltpu.PrefetchScalarGridSpec(num...]
  transfers between devices with their start and end apart: 10 -> 10, of which waited for: 3 -> 3; matrix products, arithmetic and copies ran while one was open for 1% -> 1% of each run, Pallas kernels for 12% -> 11%
where the time goes in v6:
time: 175 us
  blocking collectives  67.6 us (39%)
  starting transfers between devices  39.2 us (22%)
  waiting for transfers between devices  22.6 us (13%)
  Pallas kernels  20.7 us (12%)
  between operations  15.4 us (9%)
  local copies, waits for them, and re-layouts  7.49 us (4%)
    all_to_all x2, blocking collectives, swap(): return lax.all_to_all(array, axis, 0, 0, tiled=True)  31.4 us
    all_to_all x5, starting transfers between devices, swap(): return lax.all_to_all(array, axis, 0, 0, tiled=True)  24.2 us
    all_gather x1, blocking collectives, body(): anchors = lax.all_gather(anchors, 'l', axis=0, tiled=True)  21.2 us
    pallas_call x2, Pallas kernels, context_attention(): pl.pallas_call(context_kernel, grid_spec=pltpu.PrefetchScalarGridSpec(num...  16.2 us
    ppermute x3, starting transfers between devices, around(): got.append(lax.ppermute(block, ('h', 'l'), pairs))  15 us
    all_gather x1, blocking collectives, body(): anchors = lax.all_gather(anchors, 'h', axis=0, tiled=True)  15 us
    all_gather x1, waiting for transfers between devices, body(): anchors = lax.all_gather(anchors, 'y', axis=0, tiled=False)  12 us
    ppermute x3, waiting for transfers between devices, around(): got.append(lax.ppermute(block, ('h', 'l'), pairs))  8.7 us
  transfers between devices with their start and end apart: 10, of which 3 were waited for; matrix products, arithmetic and copies ran while one was open for 1% of the time, Pallas kernels for 11%

profile of v6, /device:TPU:1, one launch (start us, length us, event | category | flops | bytes accessed | tf_op | source)
XLA Modules:
  0.0 174.6 jit_solution(17001433622439174056)
XLA Ops:
  7.2 0.9 copy-done.2
  8.1 0.8 copy-done.4
  9.0 0.9 shard_map.95
  9.8 5.1 %all-to-all-start = ((bf16[4,512,128]{2,1,0:T(8,128)(2,1)}), bf16[4,512,128]{2,1,0:T(8,128)(2,1)S(1)}, u32[]{:S(2)}, u32[]{:S(2)}) async-start(bf16[4,512,128]{2,1,0:T(8,128)(2,1)} %shard_map.95), calls=%async_computation | async-start | bytes 1048576 | tf_op jit(solution)/shard_map/all_to_all | solution.py:199
  15.6 0.9 pad_bitcast_fusion
  16.5 3.5 %collective-permute-start = (bf16[1,528,128]{2,1,0:T(8,128)(2,1)S(1)}, bf16[1,528,128]{2,1,0:T(8,128)(2,1)S(1)}, u32[]{:S(2)}, u32[]{:S(2)}) collective-permute-start(bf16[1,528,128]{2,1,0:T(8,128)(2,1)S(1)} %pad_bitcast_fusion), channel_id=1, source_target_pairs={{0,8},{8,16},{16,24},{24,32},{32,40},{40,48},{48,56},{56,64},{64,7... | collective-permute-start | bytes 405512 | tf_op jit(solution)/shard_map/ppermute | solution.py:205
  20.1 9.5 %collective-permute-start.1 = (bf16[1,528,128]{2,1,0:T(8,128)(2,1)S(1)}, bf16[1,528,128]{2,1,0:T(8,128)(2,1)S(1)}, u32[]{:S(2)}, u32[]{:S(2)}) collective-permute-start(bf16[1,528,128]{2,1,0:T(8,128)(2,1)S(1)} %pad_bitcast_fusion), channel_id=1, source_target_pairs={{0,120},{8,0},{16,8},{24,16},{32,24},{40,32},{48,40},{56,48},{64,5... | collective-permute-start | bytes 405512 | tf_op jit(solution)/shard_map/ppermute | solution.py:205
  29.6 1.9 %collective-permute-start.2 = (bf16[1,528,128]{2,1,0:T(8,128)(2,1)S(1)}, bf16[1,528,128]{2,1,0:T(8,128)(2,1)S(1)}, u32[]{:S(2)}, u32[]{:S(2)}) collective-permute-start(bf16[1,528,128]{2,1,0:T(8,128)(2,1)S(1)} %pad_bitcast_fusion), channel_id=1, source_target_pairs={{0,16},{8,24},{16,32},{24,40},{32,48},{40,56},{48,64},{56,72},{64,... | collective-permute-start | bytes 405512 | tf_op jit(solution)/shard_map/ppermute | solution.py:205
  31.6 8.7 %collective-permute-done.2 = bf16[1,528,128]{2,1,0:T(8,128)(2,1)S(1)} collective-permute-done((bf16[1,528,128]{2,1,0:T(8,128)(2,1)S(1)}, bf16[1,528,128]{2,1,0:T(8,128)(2,1)S(1)}, u32[]{:S(2)}, u32[]{:S(2)}) %collective-permute-start.2) | collective-permute-done | bytes 135200 | tf_op jit(solution)/shard_map/ppermute | solution.py:205
  40.2 0.9 pad_maximum_fusion
  41.1 1.0 shard_map.96
  42.1 3.4 %all-to-all-start.1 = ((f32[4,64,256]{2,1,0:T(8,128)}), f32[4,64,256]{2,1,0:T(8,128)S(1)}, u32[]{:S(2)}, u32[]{:S(2)}) async-start(f32[4,64,256]{2,1,0:T(8,128)} %shard_map.96), calls=%async_computation.1 | async-start | bytes 524288 | tf_op jit(solution)/shard_map/all_to_all | solution.py:199
  45.6 15.0 %all_gather.15 = bf16[4,2,64,128]{3,2,1,0:T(8,128)(2,1)S(1)} all-gather(bf16[1,2,64,128]{3,2,1,0:T(8,128)(2,1)S(1)} %bitcast.9), channel_id=1, replica_groups=mesh['y'=4,'h'=4,'l'=4,'x'=4,'c'=2] {'h'}, dimensions={0}, use_global_device_ids=true | all-gather | bytes 163840 | tf_op jit(solution)/shard_map/all_gather | solution.py:241
  60.5 0.7 broadcast_in_dim.10
  61.3 6.4 %all-to-all-start.2 = ((f32[4,64,256]{2,1,0:T(8,128)}), f32[4,64,256]{2,1,0:T(8,128)S(1)}, u32[]{:S(2)}, u32[]{:S(2)}) async-start(f32[4,64,256]{2,1,0:T(8,128)} %broadcast_in_dim.10), calls=%async_computation.2 | async-start | bytes 524288 | tf_op jit(solution)/shard_map/all_to_all | solution.py:199
  67.6 21.2 %all_gather.16 = bf16[16,2,64,128]{3,2,1,0:T(8,128)(2,1)} all-gather(bf16[4,2,64,128]{3,2,1,0:T(8,128)(2,1)S(1)} %all_gather.15), channel_id=1, replica_groups=mesh['y'=4,'h'=4,'l'=4,'x'=4,'c'=2] {'l'}, dimensions={0}, use_global_device_ids=true | all-gather | bytes 655360 | tf_op jit(solution)/shard_map/all_gather | solution.py:244
  89.0 1.6 copy-done
  90.6 1.6 shard_map.97
  92.1 22.7 %all_to_all.35.in_ref = bf16[4,144,128]{2,1,0:T(8,128)(2,1)S(1)} all-to-all(bf16[4,144,128]{2,1,0:T(8,128)(2,1)S(1)} %shard_map.97), channel_id=1, replica_groups=mesh['y'=4,'h'=4,'l'=4,'x'=4,'c'=2] {'h'}, dimensions={0} | all-to-all | bytes 294912 | tf_op jit(solution)/shard_map/all_to_all | solution.py:199
  114.8 0.2 shard_map.98
  115.0 8.7 %all_to_all.36 = bf16[4,64,256]{2,1,0:T(8,128)(2,1)S(1)} all-to-all(bf16[4,64,256]{2,1,0:T(8,128)(2,1)S(1)} %shard_map.98), channel_id=1, replica_groups=mesh['y'=4,'h'=4,'l'=4,'x'=4,'c'=2] {'l'}, dimensions={0} | all-to-all | bytes 262144 | tf_op jit(solution)/shard_map/all_to_all | solution.py:199
  123.7 12.0 %all-gather.6.cloned.1.call-done = bf16[64,2,64,128]{3,2,1,0:T(8,128)(2,1)} async-done(((bf16[16,2,64,128]{3,2,1,0:T(8,128)(2,1)}), bf16[64,2,64,128]{3,2,1,0:T(8,128)(2,1)}) %all-gather.6.cloned.1.call-update) | async-done | bytes 2097168 | tf_op jit(solution)/shard_map/all_gather | solution.py:246
  135.7 0.9 broadcast_in_dim.22
  136.6 3.5 %all-to-all-start.5 = ((bf16[4,4,64,256]{3,2,1,0:T(8,128)(2,1)}), bf16[4,4,64,256]{3,2,1,0:T(8,128)(2,1)S(1)}, u32[]{:S(2)}, u32[]{:S(2)}) async-start(bf16[4,4,64,256]{3,2,1,0:T(8,128)(2,1)} %broadcast_in_dim.22), calls=%async_computation.5 | async-start | bytes 1048576 | tf_op jit(solution)/shard_map/all_to_all | solution.py:199
  140.7 0.1 pad_add_fusion.bounds
  140.8 1.6 copy-done.5
  142.4 4.6 %shard_map.99.rest_0_ = bf16[256,1024]{1,0:T(8,128)(2,1)} custom-call(s32[2]{0:T(128)S(1)} %pad_add_fusion.bounds, bf16[256,1024]{1,0:T(8,128)(2,1)S(1)} %copy-done.7, bf16[2,256,128]{2,1,0:T(8,128)(2,1)S(1)} %copy-done.3, bf16[4,16,2,64,128]{4,3,2,1,0:T(8,128)(2,1)S(1)} %bitcast.7), custom_call_target="tpu_custom_call" | custom-call | flops 2281701376 | bytes 2097152 | tf_op jit(solution)/shard_map/pallas_call | solution.py:69
  147.0 1.9 %all-to-all-done.5.att_ref = bf16[4,4,64,256]{3,2,1,0:T(8,128)(2,1)S(1)} async-done(((bf16[4,4,64,256]{3,2,1,0:T(8,128)(2,1)}), bf16[4,4,64,256]{3,2,1,0:T(8,128)(2,1)S(1)}, u32[]{:S(2)}, u32[]{:S(2)}) %all-to-all-start.5) | async-done | bytes 524320 | tf_op jit(solution)/shard_map/all_to_all | solution.py:199
  148.9 0.9 shard_map.100
  149.8 5.8 %all-to-all-start.6 = ((f32[8,32,128]{2,1,0:T(8,128)}), f32[8,32,128]{2,1,0:T(8,128)S(1)}, u32[]{:S(2)}, u32[]{:S(2)}) async-start(f32[8,32,128]{2,1,0:T(8,128)} %shard_map.100), calls=%async_computation.6 | async-start | bytes 262144 | tf_op jit(solution)/shard_map/all_to_all | solution.py:199
  155.6 11.6 %shard_map.101 = bf16[256,1024]{1,0:T(8,128)(2,1)} custom-call(s32[2]{0:T(128)S(1)} %pad_add_fusion.bounds, bf16[256,1024]{1,0:T(8,128)(2,1)S(1)} %copy-done.7, bf16[2,256,128]{2,1,0:T(8,128)(2,1)S(1)} %copy-done.3, bf16[4,16,2,64,128]{4,3,2,1,0:T(8,128)(2,1)S(1)} %bitcast.8, bf16[256,1024]{1,0:T(8,128)(2,1)} %shard_map.99.rest_0_), custom_call_target="tpu_custom_call", output_to_operand_aliasing={{}: (4, {})} | custom-call | flops 6845104128 | bytes 2097152 | tf_op jit(solution)/shard_map/pallas_call | solution.py:69
  167.2 0.6 reduce_sum.29
  (27 shorter events, 0.2 us)
Async XLA Ops:
  7.2 1.0 copy-start.2
  8.1 0.8 copy-start.4
  9.8 35.7 %copy-start.8 = (bf16[2,64,128]{2,1,0:T(8,128)(2,1)S(1)}, bf16[2,64,128]{2,1,0:T(8,128)(2,1)}, u32[]{:S(2)}) copy-start(bf16[2,64,128]{2,1,0:T(8,128)(2,1)} %param.10) | copy-start | bytes 98308
  9.8 30.4 %all-to-all-start = ((bf16[4,512,128]{2,1,0:T(8,128)(2,1)}), bf16[4,512,128]{2,1,0:T(8,128)(2,1)S(1)}, u32[]{:S(2)}, u32[]{:S(2)}) async-start(bf16[4,512,128]{2,1,0:T(8,128)(2,1)} %shard_map.95), calls=%async_computation | async-start | bytes 1048576 | tf_op jit(solution)/shard_map/all_to_all | solution.py:199
  15.0 74.0 %all-gather.4.cloned.1.call-start = ((), (), s32[]{:S(2)}) async-start(), calls=%async_computation.7 | async-start | bytes 2703360 | tf_op jit(solution)/shard_map/all_gather | solution.py:234
  16.5 15.0 %collective-permute-start = (bf16[1,528,128]{2,1,0:T(8,128)(2,1)S(1)}, bf16[1,528,128]{2,1,0:T(8,128)(2,1)S(1)}, u32[]{:S(2)}, u32[]{:S(2)}) collective-permute-start(bf16[1,528,128]{2,1,0:T(8,128)(2,1)S(1)} %pad_bitcast_fusion), channel_id=1, source_target_pairs={{0,8},{8,16},{16,24},{24,32},{32,40},{40,48},{48,56},{56,64},{64,7... | collective-permute-start | bytes 405512 | tf_op jit(solution)/shard_map/ppermute | solution.py:205
  20.1 11.5 %collective-permute-start.1 = (bf16[1,528,128]{2,1,0:T(8,128)(2,1)S(1)}, bf16[1,528,128]{2,1,0:T(8,128)(2,1)S(1)}, u32[]{:S(2)}, u32[]{:S(2)}) collective-permute-start(bf16[1,528,128]{2,1,0:T(8,128)(2,1)S(1)} %pad_bitcast_fusion), channel_id=1, source_target_pairs={{0,120},{8,0},{16,8},{24,16},{32,24},{40,32},{48,40},{56,48},{64,5... | collective-permute-start | bytes 405512 | tf_op jit(solution)/shard_map/ppermute | solution.py:205
  29.6 10.6 %collective-permute-start.2 = (bf16[1,528,128]{2,1,0:T(8,128)(2,1)S(1)}, bf16[1,528,128]{2,1,0:T(8,128)(2,1)S(1)}, u32[]{:S(2)}, u32[]{:S(2)}) collective-permute-start(bf16[1,528,128]{2,1,0:T(8,128)(2,1)S(1)} %pad_bitcast_fusion), channel_id=1, source_target_pairs={{0,16},{8,24},{16,32},{24,40},{32,48},{40,56},{48,64},{56,72},{64,... | collective-permute-start | bytes 405512 | tf_op jit(solution)/shard_map/ppermute | solution.py:205
  42.1 18.4 %all-to-all-start.1 = ((f32[4,64,256]{2,1,0:T(8,128)}), f32[4,64,256]{2,1,0:T(8,128)S(1)}, u32[]{:S(2)}, u32[]{:S(2)}) async-start(f32[4,64,256]{2,1,0:T(8,128)} %shard_map.96), calls=%async_computation.1 | async-start | bytes 524288 | tf_op jit(solution)/shard_map/all_to_all | solution.py:199
  61.3 27.6 %all-to-all-start.2 = ((f32[4,64,256]{2,1,0:T(8,128)}), f32[4,64,256]{2,1,0:T(8,128)S(1)}, u32[]{:S(2)}, u32[]{:S(2)}) async-start(f32[4,64,256]{2,1,0:T(8,128)} %broadcast_in_dim.10), calls=%async_computation.2 | async-start | bytes 524288 | tf_op jit(solution)/shard_map/all_to_all | solution.py:199
  67.6 68.1 %all-gather.6.cloned.1.call-start = ((), (), s32[]{:S(2)}) async-start(), calls=%async_computation.8 | async-start | bytes 2621440 | tf_op jit(solution)/shard_map/all_gather | solution.py:246
  89.0 1.6 copy-start
  90.6 50.2 %copy-start.3 = (bf16[2,256,128]{2,1,0:T(8,128)(2,1)S(1)}, bf16[2,256,128]{2,1,0:T(8,128)(2,1)}, u32[]{:S(2)}) copy-start(bf16[2,256,128]{2,1,0:T(8,128)(2,1)} %own_ref.3) | copy-start | bytes 393220
  90.6 50.2 %copy-start.7 = (bf16[256,1024]{1,0:T(8,128)(2,1)S(1)}, bf16[256,1024]{1,0:T(8,128)(2,1)}, u32[]{:S(2)}) copy-start(bf16[256,1024]{1,0:T(8,128)(2,1)} %q_ref.5) | copy-start | bytes 1572868
  136.6 12.3 %all-to-all-start.5 = ((bf16[4,4,64,256]{3,2,1,0:T(8,128)(2,1)}), bf16[4,4,64,256]{3,2,1,0:T(8,128)(2,1)S(1)}, u32[]{:S(2)}, u32[]{:S(2)}) async-start(bf16[4,4,64,256]{3,2,1,0:T(8,128)(2,1)} %broadcast_in_dim.22), calls=%async_computation.5 | async-start | bytes 1048576 | tf_op jit(solution)/shard_map/all_to_all | solution.py:199
  140.8 1.6 copy-start.5
  142.4 6.5 %copy-start.1 = (bf16[1024,128]{1,0:T(8,128)(2,1)S(1)}, bf16[1024,128]{1,0:T(8,128)(2,1)}, u32[]{:S(2)}) copy-start(bf16[1024,128]{1,0:T(8,128)(2,1)} %w_ref.3) | copy-start | bytes 786436
  142.4 13.3 %copy-start.6 = (bf16[64,2,64,128]{3,2,1,0:T(8,128)(2,1)S(1)}, bf16[64,2,64,128]{3,2,1,0:T(8,128)(2,1)}, u32[]{:S(2)}) copy-start(bf16[64,2,64,128]{3,2,1,0:T(8,128)(2,1)} %all-gather.6.cloned.1.call-done) | copy-start | bytes 6291460
  149.8 17.4 %all-to-all-start.6 = ((f32[8,32,128]{2,1,0:T(8,128)}), f32[8,32,128]{2,1,0:T(8,128)S(1)}, u32[]{:S(2)}, u32[]{:S(2)}) async-start(f32[8,32,128]{2,1,0:T(8,128)} %shard_map.100), calls=%async_computation.6 | async-start | bytes 262144 | tf_op jit(solution)/shard_map/all_to_all | solution.py:199
Sparse Core Ops, SparseCore 0:
  41.3 37.6 all-gather.3
  89.0 46.6 all-gather.5
